TPU v7x, 1024 devices: a whole 4x4x32 slice. The times are simulated.
1024 devices in a mesh: half: 2 (over core), dp: 16 (over x, y), tensor: 32 (over z).
Axes of the slice: x: 4, y: 4, z: 32, core: 2. Of those that a mesh axis runs over, the one named last changes fastest.
Arguments:
- history: bfloat16 [16, 128, 512, 1024], P('dp', ('half', 'tensor')), may hold values from -6 to 6
- queries: bfloat16 [16, 128, 64, 1024], P('dp', ('half', 'tensor'))
- lengths: int32 [16, 128], P('dp', ('half', 'tensor')), may hold values from 128 to 512, as said below
- assignment: int32 [16, 128], P('dp'), may hold values from 0 to 127, each once within a row
- key_weight: bfloat16 [1024, 1024], replicated, may hold values from -0.1875 to 0.1875
- key_gain: float32 [1024], replicated, may hold values from 0.5 to 2
- interest_gain: float32 [256], replicated, may hold values from 0.5 to 2
- sparse_embed: bfloat16 [2048, 256, 256], P('dp', ('half', 'tensor')), may hold values from -6 to 6
- proj_interest: bfloat16 [256, 12], P(('half', 'tensor')), may hold values from -0.25 to 0.25
- proj_sparse: bfloat16 [256, 12], P(('half', 'tensor')), may hold values from -0.25 to 0.25
- cot_interest: bfloat16 [2048, 256, 12], P('dp', ('half', 'tensor')), may hold values from -6 to 6
- cot_sparse: bfloat16 [2048, 256, 12], P('dp', ('half', 'tensor')), may hold values from -6 to 6
Outputs:
- grad_interest: bfloat16 [2048, 256, 256], P('dp', ('half', 'tensor'))
- grad_sparse: bfloat16 [2048, 256, 256], P('dp', ('half', 'tensor'))
- grad_proj_interest: float32 [256, 12], P(('half', 'tensor'))
- grad_proj_sparse: float32 [256, 12], P(('half', 'tensor'))
Inputs may be any that keep to these rules, and one draw needn't show every extreme that they name: `lengths`: every length is a multiple of 128; in every batch shard some user has exactly 512.
All inputs are finite; a program needn't handle non-finite values.
Results may differ from a plain program's by a relative error of at most 0.0085.
Values may be sent and summed in bfloat16 or wider, within the bound.
No kernel may reach another device: no remote copies, remote signals or barrier semaphores. Data moves between devices by JAX's collectives and lax.ppermute only.
A program may use at most 32 MiB of HBM per device.

v0:
```python
import functools
import math

import jax
import jax.numpy as jnp
from jax import lax
from jax.experimental import pallas as pl
from jax.experimental.pallas import tpu as pltpu
from jax.sharding import PartitionSpec as P

HEADS = 8
EMB = 256
RANK = 12
STATE = 2 * RANK
SIDE = 2 * EMB
PACKED = 2 * EMB + 128
NEAR = 4
PAIR = 2
ALL = ("half", "tensor")
F32 = jnp.float32
BF16 = jnp.bfloat16


def key_rows(history_rows, key_weight, key_gain):
    raw_keys = jnp.dot(history_rows, key_weight, preferred_element_type=F32)
    row_count, model_width = raw_keys.shape
    by_head = raw_keys.reshape(row_count, HEADS, model_width // HEADS)
    shrink = lax.rsqrt(jnp.mean(by_head * by_head, axis=-1, keepdims=True) + 1e-06)
    return ((by_head * shrink).reshape(row_count, model_width) * key_gain).astype(BF16)


def encode_user(history_rows, user_query, user_length, key_weight, key_gain, interest_gain):
    seq_len, model_width = history_rows.shape
    head_dim = model_width // HEADS
    key_block = key_rows(history_rows, key_weight, key_gain)
    query_heads = user_query.reshape(user_query.shape[0], HEADS, head_dim)
    key_heads = key_block.reshape(seq_len, HEADS, head_dim)
    scores = jnp.einsum(
        "qhd,lhd->hql", query_heads, key_heads, preferred_element_type=F32
    ) / math.sqrt(head_dim)
    live_mask = lax.broadcasted_iota(jnp.int32, (1, 1, seq_len), 2) < user_length
    scores = jnp.where(live_mask, scores, -1e30)
    row_max = jnp.max(scores, axis=-1, keepdims=True)
    expo = jnp.exp(scores - row_max)
    attention = (expo / jnp.sum(expo, axis=-1, keepdims=True)).astype(BF16)
    value_heads = history_rows.reshape(seq_len, HEADS, head_dim)
    pooled = jnp.einsum("hql,lhd->qhd", attention, value_heads, preferred_element_type=F32)
    pieces = pooled.reshape(user_query.shape[0], model_width // EMB, EMB)
    norm_inv = lax.rsqrt(jnp.mean(pieces * pieces, axis=-1, keepdims=True) + 1e-06)
    normed = pieces * norm_inv * interest_gain
    return normed.reshape(user_query.shape[0] * (model_width // EMB), EMB).astype(BF16)


def pack_kernel(rows_ref, *refs):
    inputs, (out_ref, scratch), (held, arrived) = refs[:6], refs[6:8], (refs[8:14], refs[14])
    copies = [
        pltpu.make_async_copy(source, target, arrived.at[i])
        for i, (source, target) in enumerate(zip(inputs, held))
    ]
    for copy in copies:
        copy.start()
    for copy in copies:
        copy.wait()
    wanted_ref, sparse_ref, cot_int_ref, cot_spa_ref, proj_int_ref, proj_spa_ref = held
    devices, width = out_ref.shape[0], sparse_ref.shape[1]
    batch = sparse_ref.shape[0]
    for user in range(2 * devices):
        lanes = slice((user % 2) * EMB, (user % 2 + 1) * EMB)
        out_ref[user // 2, :, lanes] = sparse_ref[rows_ref[0, user]]
    row_of = lax.broadcasted_iota(jnp.int32, (batch, batch), 0)
    pick = (row_of == wanted_ref[...]).astype(BF16)
    for j in range(width):
        cots = jnp.concatenate([cot_int_ref[:, j, :], cot_spa_ref[:, j, :]], axis=0)
        scratch[:, :STATE] = lax.dot_general(
            pick, cots, (((0,), (1,)), ((), ())), preferred_element_type=F32
        )
        proj = jnp.concatenate([proj_int_ref[j : j + 1, :], proj_spa_ref[j : j + 1, :]], axis=1)
        parts = [scratch[pl.ds(slot, devices, stride=2), :STATE] for slot in range(2)]
        parts.append(jnp.broadcast_to(proj.astype(F32), (devices, STATE)))
        parts.append(jnp.zeros((devices, 128 - 3 * STATE), F32))
        out_ref[:, j, SIDE:] = jnp.concatenate(parts, axis=1).astype(BF16)


def pack(assignment, sparse_embed, cots, projs):
    batch, width, _ = sparse_embed.shape
    inputs = [
        pltpu.with_memory_space_constraint(array, pltpu.HBM)
        for array in (assignment, sparse_embed, *cots, *projs)
    ]
    return pl.pallas_call(
        pack_kernel,
        out_shape=jax.ShapeDtypeStruct((batch // 2, width, PACKED), BF16),
        in_specs=[pl.BlockSpec(memory_space=pltpu.SMEM)]
        + [pl.BlockSpec(memory_space=pltpu.HBM)] * len(inputs),
        out_specs=pl.BlockSpec(memory_space=pltpu.VMEM),
        scratch_shapes=[pltpu.VMEM((batch, 128), F32)]
        + [pltpu.VMEM(array.shape, array.dtype) for array in inputs]
        + [pltpu.SemaphoreType.DMA((len(inputs),))],
        compiler_params=pltpu.CompilerParams(vmem_limit_bytes=32 * 2**20),
        name="pack_rows",
    )(assignment, *inputs)


def state_kernel(factor, packed_ref, interest_ref, sent_ref):
    contract_rows = (((0,), (0,)), ((), ()))
    contract_lanes = (((1,), (1,)), ((), ()))
    side = packed_ref[:, SIDE:]
    proj = side[:, 2 * STATE : 3 * STATE]
    total_int, total_spa = None, None
    for slot in range(2):
        interest = interest_ref[slot]
        sparse = packed_ref[:, slot * EMB : (slot + 1) * EMB]
        cot = side[:, slot * STATE : (slot + 1) * STATE]
        left_int = jnp.concatenate([proj[:, :RANK], cot[:, :RANK]], axis=1)
        left_spa = jnp.concatenate([proj[:, RANK:], cot[:, RANK:]], axis=1)
        summed = lax.dot_general(
            left_int, interest, contract_rows, preferred_element_type=F32
        ) + lax.dot_general(left_spa, sparse, contract_rows, preferred_element_type=F32)
        is_state = lax.broadcasted_iota(jnp.int32, summed.shape, 0) < RANK
        rounded = jnp.where(is_state, summed, summed * factor).astype(BF16)
        sent_ref[slot] = rounded
        grad = rounded[RANK:, :]
        part_int = lax.dot_general(grad, interest, contract_lanes, preferred_element_type=F32)
        part_spa = lax.dot_general(grad, sparse, contract_lanes, preferred_element_type=F32)
        total_int = part_int if total_int is None else total_int + part_int
        total_spa = part_spa if total_spa is None else total_spa + part_spa
    sent_ref[2] = jnp.concatenate([total_int, total_spa], axis=0).astype(BF16)


def make_state(packed, interest):
    vmem = pl.BlockSpec(memory_space=pltpu.VMEM)
    return pl.pallas_call(
        functools.partial(state_kernel, 1.0 / math.sqrt(EMB)),
        out_shape=jax.ShapeDtypeStruct((3, STATE, EMB), BF16),
        in_specs=[vmem, vmem],
        out_specs=vmem,
        compiler_params=pltpu.CompilerParams(vmem_limit_bytes=32 * 2**20),
        name="make_state",
    )(packed, interest)


def split_kernel(shards, block_ref, got_ref, state_ref, spread_ref):
    total = None
    for source in range(state_ref.shape[0]):
        for slot in range(2):
            state_ref[source, slot * STATE : (slot + 1) * STATE, :] = got_ref[3 * source + slot]
        part = got_ref[3 * source + 2].astype(F32)
        total = part if total is None else total + part
    total = jnp.concatenate([total, jnp.zeros((128 - STATE, total.shape[1]), F32)], axis=0)
    width = spread_ref.shape[1]
    halves = 2
    columns = total.shape[1] // halves
    for half in range(halves):
        mine = pltpu.roll(
            total[:, half * columns : (half + 1) * columns],
            columns - block_ref[0] * PAIR * width,
            1,
        )
        turned = jnp.transpose(mine)
        for member in range(PAIR):
            row = turned[member * width : (member + 1) * width, :]
            for shard in range(shards):
                spread_ref[(half * shards + shard) * PAIR + member] = row


def split_sums(block, gathered, shards, width):
    vmem = pl.BlockSpec(memory_space=pltpu.VMEM)
    sources, emb = gathered.shape[0] // 3, gathered.shape[2]
    return pl.pallas_call(
        functools.partial(split_kernel, shards),
        out_shape=(
            jax.ShapeDtypeStruct((sources, 2 * STATE, emb), BF16),
            jax.ShapeDtypeStruct((2 * shards * PAIR, width, 128), F32),
        ),
        in_specs=[pl.BlockSpec(memory_space=pltpu.SMEM), vmem],
        out_specs=(vmem, vmem),
        compiler_params=pltpu.CompilerParams(vmem_limit_bytes=32 * 2**20),
        name="split_sums",
    )(block, gathered)


def embed_kernel(rows_ref, left_int_ref, left_spa_ref, *refs):
    sources, (int_ref, spa_ref) = refs[:-2], refs[-2:]
    each = left_int_ref.shape[0] // len(sources)
    for block in range(left_int_ref.shape[0]):
        source = sources[block // each]
        first = (block % each) * NEAR
        states = source[first : first + NEAR].reshape(NEAR * 2 * STATE, EMB)
        got_int = jnp.dot(left_int_ref[block], states, preferred_element_type=F32)
        got_spa = jnp.dot(left_spa_ref[block], states, preferred_element_type=F32)
        for i in range(2 * NEAR):
            row = rows_ref[block * 2 * NEAR + i]
            int_ref[row] = got_int[8 * i : 8 * i + 4, :].astype(BF16)
            spa_ref[row] = got_spa[8 * i : 8 * i + 4, :].astype(BF16)


def embed_grads(rows, left_int, left_spa, sources, width):
    vmem = pl.BlockSpec(memory_space=pltpu.VMEM)
    out = jax.ShapeDtypeStruct((rows.shape[0], width, EMB), BF16)
    return pl.pallas_call(
        embed_kernel,
        out_shape=(out, out),
        in_specs=[pl.BlockSpec(memory_space=pltpu.SMEM)] + [vmem] * (2 + len(sources)),
        out_specs=(vmem, vmem),
        compiler_params=pltpu.CompilerParams(vmem_limit_bytes=32 * 2**20),
        name="embed_grads",
    )(rows, left_int, left_spa, *sources)


def left_kernel(
    factor, wanted_ref, cot_int_ref, cot_spa_ref, proj_int_ref, proj_spa_ref, left_int_ref, left_spa_ref, rows
):
    blocks, height, depth = left_int_ref.shape
    users, width = wanted_ref.shape[1], proj_int_ref.shape[0]
    row_of = lax.broadcasted_iota(jnp.int32, (users, users), 0)
    pick = (row_of == wanted_ref[...]).astype(BF16)
    same = lax.broadcasted_iota(jnp.int32, (STATE, STATE), 0) == lax.broadcasted_iota(
        jnp.int32, (STATE, STATE), 1
    )
    repeat = jnp.concatenate([same.astype(BF16)] * (depth // STATE), axis=1)
    owner = lax.broadcasted_iota(jnp.int32, (height, STATE), 0) // 8
    mask = jnp.concatenate([(owner == i).astype(F32) for i in range(depth // STATE)], axis=1)
    for cot_ref, proj_ref, left_ref in (
        (cot_int_ref, proj_int_ref, left_int_ref),
        (cot_spa_ref, proj_spa_ref, left_spa_ref),
    ):
        rows[...] = jnp.zeros_like(rows)
        for j in range(width):
            cot = lax.dot_general(
                pick, cot_ref[:, j, :], (((0,), (1,)), ((), ())), preferred_element_type=F32
            )
            proj = jnp.broadcast_to(proj_ref[j : j + 1, :].astype(F32), (users, RANK))
            row = [cot * factor, proj, jnp.zeros((users, 128 - STATE), F32)]
            rows[pl.ds(j, users, stride=8), :] = jnp.concatenate(row, axis=1)
        for block in range(blocks):
            narrow = rows[block * height : (block + 1) * height, :STATE].astype(BF16)
            wide = jnp.dot(narrow, repeat, preferred_element_type=F32)
            left_ref[block] = (wide * mask).astype(BF16)


def left_blocks(wanted, cots, projs, factor):
    vmem = pl.BlockSpec(memory_space=pltpu.VMEM)
    users = wanted.shape[1]
    per_block = 2 * NEAR
    out = jax.ShapeDtypeStruct((users // per_block, per_block * 8, per_block * STATE), BF16)
    return pl.pallas_call(
        functools.partial(left_kernel, factor),
        out_shape=(out, out),
        in_specs=[vmem] * 5,
        out_specs=(vmem, vmem),
        scratch_shapes=[pltpu.VMEM((users * 8, 128), F32)],
        compiler_params=pltpu.CompilerParams(vmem_limit_bytes=32 * 2**20),
        name="left_blocks",
    )(wanted, *cots, *projs)


def on_device(
    history,
    queries,
    lengths,
    assignment,
    key_weight,
    key_gain,
    interest_gain,
    sparse_embed,
    proj_interest,
    proj_sparse,
    cot_interest,
    cot_sparse,
):
    batch_rows = assignment[0]
    batch_local, width, _ = sparse_embed.shape
    devices = batch_local // 2
    tensor = lax.axis_size("tensor")
    halves = lax.axis_size("half")
    factor = 1.0 / math.sqrt(EMB)

    cots = [cot_interest.transpose(2, 1, 0), cot_sparse.transpose(2, 1, 0)]
    packed = pack(assignment, sparse_embed, cots, [proj_interest, proj_sparse])
    arrived = lax.all_to_all(packed, ALL, split_axis=0, concat_axis=0, tiled=True)

    user_count = history.shape[1]
    encoded = [
        encode_user(
            history[0, user_slot],
            queries[0, user_slot],
            lengths[0, user_slot],
            key_weight,
            key_gain,
            interest_gain,
        )
        for user_slot in range(user_count)
    ]
    interest = jnp.stack(encoded, axis=0)

    far_count = tensor // PAIR
    far_groups = [[i + PAIR * m for m in range(far_count)] for i in range(PAIR)]
    my_half = lax.axis_index("half")
    my_tensor = lax.axis_index("tensor")
    tables = batch_rows.reshape(halves, far_count, PAIR, 2).transpose(0, 2, 1, 3)
    tables = jnp.where(my_half == 0, tables, tables[::-1])
    tables = jnp.where(my_tensor % PAIR == 0, tables, tables[:, ::-1])
    ordered_rows = tables.reshape(batch_local)
    left_int, left_spa = left_blocks(
        ordered_rows[None], cots, [proj_interest, proj_sparse], factor
    )
    interest, left_int, left_spa = lax.optimization_barrier((interest, left_int, left_spa))

    sent = make_state(arrived.reshape(devices * width, PACKED), interest)
    gathered = lax.all_gather(sent, "tensor", axis=0, tiled=True, axis_index_groups=far_groups)

    shards = lax.axis_size("dp")
    pair = my_tensor // PAIR
    far, spread = split_sums(pair.reshape(1).astype(jnp.int32), gathered, shards, width)
    across = [(i, (i + 1) % halves) for i in range(halves)]
    swap = [(i, i ^ 1) for i in range(tensor)]
    near = lax.ppermute(far, "tensor", swap)
    far_other = lax.ppermute(far, "half", across)
    near_other = lax.ppermute(near, "half", across)
    sum_groups = [
        [
            (half * shards + shard) * tensor + PAIR * m + i
            for half in range(halves)
            for shard in range(shards)
            for i in range(PAIR)
        ]
        for m in range(far_count)
    ]
    shares = lax.all_to_all(
        spread,
        ("half", "dp", "tensor"),
        split_axis=0,
        concat_axis=0,
        tiled=True,
        axis_index_groups=sum_groups,
    )
    batch_total = shards * batch_local
    proj_grads = jnp.sum(shares, axis=0)[:, :STATE] / batch_total

    grad_interest, grad_sparse = embed_grads(
        ordered_rows, left_int, left_spa, [far, near, far_other, near_other], width
    )
    return (grad_interest, grad_sparse, proj_grads[:, :RANK], proj_grads[:, RANK:])


def solution(mesh):
    placed = (
        P("dp", ("half", "tensor"), None, None),
        P("dp", ("half", "tensor"), None, None),
        P("dp", ("half", "tensor")),
        P("dp", None),
        P(),
        P(),
        P(),
        P("dp", ("half", "tensor"), None),
        P(("half", "tensor"), None),
        P(("half", "tensor"), None),
        P("dp", ("half", "tensor"), None),
        P("dp", ("half", "tensor"), None),
    )
    return jax.shard_map(
        on_device,
        mesh=mesh,
        in_specs=placed,
        out_specs=(
            P("dp", ("half", "tensor"), None),
            P("dp", ("half", "tensor"), None),
            P(("half", "tensor"), None),
            P(("half", "tensor"), None),
        ),
        check_vma=False,
    )
```

profile of v0, /device:TPU:1, one launch (start us, length us, event | category | flops | bytes accessed | tf_op | source)
XLA Modules:
  0.0 144.5 jit_solution(15409510336572947985)
XLA Ops:
  0.6 2.9 %pack_rows.1 = bf16[64,4,640]{2,1,0:T(4,128)(2,1)} custom-call(s32[1,128]{1,0:T(1,128)} %refs_0_.1, s32[1,128]{1,0:T(1,128)} %refs_0_.1, bf16[128,4,256]{2,1,0:T(4,128)(2,1)} %refs_1_.1, bf16[12,4,128]{2,1,0:T(4,128)(2,1)} %bitcast.63, bf16[12,4,128]{2,1,0:T(4,128)(2,1)} %bitcast.65, bf16[4,12]{1,0:T(4,128)(2,1)} %refs_4_.1, bf16[4,12]{1,0:T(4,128)(2,1)} %refs_5_.1), custom_call_target="tpu_custom_call" | custom-call | tf_op jit(solution)/shard_map/pack_rows/pallas_call | solution.py:90
  3.6 30.5 %all-to-all-start = ((bf16[64,4,640]{2,1,0:T(4,128)(2,1)}), bf16[64,4,640]{2,1,0:T(4,128)(2,1)S(1)}, u32[]{:S(2)}, u32[]{:S(2)}) async-start(bf16[64,4,640]{2,1,0:T(4,128)(2,1)} %pack_rows.1), calls=%async_computation | async-start | bytes 655360 | tf_op jit(solution)/shard_map/all_to_all | solution.py:280
  34.6 1.3 reduce.7
  39.2 0.8 left_blocks.1
  40.0 4.0 %copy.54 = bf16[1024,1024]{1,0:T(8,128)(2,1)} copy(bf16[1024,1024]{0,1:T(8,128)(2,1)} %bitcast.67) | data formatting | bytes 4194304 | tf_op jit(solution)/shard_map/dot_general | solution.py:25
  43.9 1.9 %slice_bitcast_fusion.1 = (bf16[64,8,8,128]{3,1,2,0:T(8,128)(2,1)S(1)}, bf16[64,8,8,128]{3,1,2,0:T(8,128)(2,1)S(1)}) fusion(bf16[1,2,512,1024]{3,2,1,0:T(8,128)(2,1)} %param.12), kind=kLoop, calls=%fused_computation.32 | loop fusion | bytes 4194304
  46.8 1.3 multiply_reduce_fusion
  50.1 1.3 copy.58
  52.1 3.0 %multiply_reduce_fusion.2 = (f32[64,8]{0,1:T(8,128)S(1)}, f32[64,8,128]{2,0,1:T(8,128)}) fusion(bf16[512,8,128]{2,1,0:T(8,128)(2,1)} %bitcast.71, f32[8,64]{1,0:T(8,128)S(1)} %fusion.31, f32[8,64,512]{2,1,0:T(8,128)S(1)} %fusion.9), kind=kOutput, calls=%fused_computation.38 | convolution fusion | flops 68026880 | bytes 2363392 | tf_op jit(solution)/shard_map/hql,lhd->qhd/dot_general | solution.py:47
  55.1 1.1 copy.49
  57.2 1.1 copy.55
  59.2 2.9 %multiply_reduce_fusion.1 = (f32[512,8]{0,1:T(8,128)S(1)}, f32[512,8,128]{0,2,1:T(8,128)S(1)}) fusion(bf16[8,128,1024]{2,1,0:T(8,128)(2,1)} %bitcast.68, bf16[1,2,512,1024]{3,2,1,0:T(8,128)(2,1)S(1)} %copy-done.5), kind=kOutput, calls=%fused_computation.5 | convolution fusion | flops 1074786304 | bytes 5259264 | tf_op jit(solution)/shard_map/dot_general | solution.py:25
  62.9 1.8 %multiply_reduce_fusion.3 = (f32[64,8]{0,1:T(8,128)S(1)}, f32[64,8,128]{2,0,1:T(8,128)}) fusion(bf16[512,8,128]{2,1,0:T(8,128)(2,1)S(1)} %bitcast.70, f32[8,64]{1,0:T(8,128)S(1)} %fusion.30, f32[8,64,512]{2,1,0:T(8,128)S(1)} %fusion.7), kind=kOutput, calls=%fused_computation.40 | convolution fusion | flops 68026880 | bytes 2363392 | tf_op jit(solution)/shard_map/hql,lhd->qhd/dot_general | solution.py:47
  64.7 1.1 copy.43
  66.1 1.1 multiply_convert_fusion.5
  67.2 9.5 %all-to-all-done = bf16[64,4,640]{2,1,0:T(4,128)(2,1)S(1)} async-done(((bf16[64,4,640]{2,1,0:T(4,128)(2,1)}), bf16[64,4,640]{2,1,0:T(4,128)(2,1)S(1)}, u32[]{:S(2)}, u32[]{:S(2)}) %all-to-all-start) | async-done | bytes 327712 | tf_op jit(solution)/shard_map/all_to_all | solution.py:280
  77.3 31.2 %all_gather.3.got_ref = bf16[48,24,256]{2,1,0:T(8,128)(2,1)S(1)} all-gather(bf16[3,24,256]{2,1,0:T(8,128)(2,1)S(1)} %make_state.1), channel_id=1, replica_groups={{0,2,4,6,8,10,12,14,16,18,20,22,24,26,28,30},{1,3,5,7,9,11,13,15,17,19,..., dimensions={0}, use_global_device_ids=true | all-gather | bytes 626688 | tf_op jit(solution)/shard_map/all_gather | solution.py:310
  109.4 15.7 %all-to-all-start.1 = ((f32[64,4,128]{2,1,0:T(4,128)}), f32[64,4,128]{2,1,0:T(4,128)S(1)}, u32[]{:S(2)}, u32[]{:S(2)}) async-start(f32[64,4,128]{2,1,0:T(4,128)} %get-tuple-element.21), calls=%async_computation.1 | async-start | bytes 262144 | tf_op jit(solution)/shard_map/all_to_all | solution.py:329
  125.0 3.3 %collective-permute-start = (bf16[16,48,256]{2,1,0:T(8,128)(2,1)S(1)}, bf16[16,48,256]{2,1,0:T(8,128)(2,1)S(1)}, u32[]{:S(2)}, u32[]{:S(2)}) collective-permute-start(bf16[16,48,256]{2,1,0:T(8,128)(2,1)S(1)} %get-tuple-element.18.refs_0_), channel_id=1, source_target_pairs={{0,1},{1,0},{2,3},{3,2},{4,5},{5,4},{6,7},{7,6},{8,9},{9,8},{10,11... | collective-permute-start | bytes 1179656 | tf_op jit(solution)/shard_map/ppermute | solution.py:317
  128.3 2.5 %collective-permute-start.1 = (bf16[16,48,256]{2,1,0:T(8,128)(2,1)S(1)}, bf16[16,48,256]{2,1,0:T(8,128)(2,1)S(1)}, u32[]{:S(2)}, u32[]{:S(2)}) collective-permute-start(bf16[16,48,256]{2,1,0:T(8,128)(2,1)S(1)} %get-tuple-element.18.refs_0_), channel_id=1, source_target_pairs={{0,512},{512,0},{1,513},{513,1},{2,514},{514,2},{3,515},{515,3},{4... | collective-permute-start | bytes 1179656 | tf_op jit(solution)/shard_map/ppermute | solution.py:318
  130.8 6.5 %collective-permute-done.refs_1_ = bf16[16,48,256]{2,1,0:T(8,128)(2,1)S(1)} collective-permute-done((bf16[16,48,256]{2,1,0:T(8,128)(2,1)S(1)}, bf16[16,48,256]{2,1,0:T(8,128)(2,1)S(1)}, u32[]{:S(2)}, u32[]{:S(2)}) %collective-permute-start) | collective-permute-done | bytes 393248 | tf_op jit(solution)/shard_map/ppermute | solution.py:317
  137.3 3.1 %collective-permute-start.2 = (bf16[16,48,256]{2,1,0:T(8,128)(2,1)S(1)}, bf16[16,48,256]{2,1,0:T(8,128)(2,1)S(1)}, u32[]{:S(2)}, u32[]{:S(2)}) collective-permute-start(bf16[16,48,256]{2,1,0:T(8,128)(2,1)S(1)} %collective-permute-done.refs_1_), channel_id=1, source_target_pairs={{0,512},{512,0},{1,513},{513,1},{2,514},{514,2},{3,515},{515,3},{4... | collective-permute-start | bytes 1179656 | tf_op jit(solution)/shard_map/ppermute | solution.py:319
  140.5 1.2 collective-permute-done.2.refs_3_
  141.7 2.0 %embed_grads.1 = (bf16[128,4,256]{2,1,0:T(4,128)(2,1)}, bf16[128,4,256]{2,1,0:T(4,128)(2,1)}) custom-call(s32[128]{0:T(128)S(1)} %reshape.221.rows_ref, bf16[16,64,192]{2,1,0:T(8,128)(2,1)S(1)} %get-tuple-element.15.left_int_ref, bf16[16,64,192]{2,1,0:T(8,128)(2,1)S(1)} %get-tuple-element.16.left_spa_ref, ...), custom_call_target="tpu_custom_call" | custom-call | tf_op jit(solution)/shard_map/embed_grads/pallas_call | solution.py:200
  (61 shorter events, 12.6 us)
Async XLA Ops:
  3.6 73.2 %all-to-all-start = ((bf16[64,4,640]{2,1,0:T(4,128)(2,1)}), bf16[64,4,640]{2,1,0:T(4,128)(2,1)S(1)}, u32[]{:S(2)}, u32[]{:S(2)}) async-start(bf16[64,4,640]{2,1,0:T(4,128)(2,1)} %pack_rows.1), calls=%async_computation | async-start | bytes 655360 | tf_op jit(solution)/shard_map/all_to_all | solution.py:280
  36.4 0.7 copy-start
  37.1 0.7 copy-start.1
  37.8 0.7 copy-start.2
  38.5 0.7 copy-start.3
  43.9 2.2 %copy-start.4 = (bf16[1,2,512,1024]{3,2,1,0:T(8,128)(2,1)S(1)}, bf16[1,2,512,1024]{3,2,1,0:T(8,128)(2,1)}, u32[]{:S(2)}) copy-start(bf16[1,2,512,1024]{3,2,1,0:T(8,128)(2,1)} %param.12) | copy-start | bytes 6291460
  43.9 2.9 %copy-start.6 = (bf16[1024,1024]{1,0:T(8,128)(2,1)S(1)}, bf16[1024,1024]{1,0:T(8,128)(2,1)}, u32[]{:S(2)}) copy-start(bf16[1024,1024]{1,0:T(8,128)(2,1)} %copy.54) | copy-start | bytes 6291460
  46.8 1.3 copy-start.7
  46.8 2.0 %copy-start.9 = (s32[1,2]{1,0:T(1,128)S(1)}, s32[1,2]{1,0:T(1,128)}, u32[]{:S(2)}) copy-start(s32[1,2]{1,0:T(1,128)} %param.14) | copy-start | bytes 28
  48.1 3.2 %copy-start.8 = (f32[1024]{0:T(1024)S(1)}, f32[1024]{0:T(1024)}, u32[]{:S(2)}) copy-start(f32[1024]{0:T(1024)} %param.17) | copy-start | bytes 12292
  57.2 2.0 %copy-start.5 = (bf16[1,2,512,1024]{3,2,1,0:T(8,128)(2,1)S(1)}, bf16[1,2,512,1024]{3,2,1,0:T(8,128)(2,1)}, u32[]{:S(2)}) copy-start(bf16[1,2,512,1024]{3,2,1,0:T(8,128)(2,1)} %param.12) | copy-start | bytes 6291460
  62.9 3.2 %copy-start.10 = (f32[256]{0:T(256)S(1)}, f32[256]{0:T(256)}, u32[]{:S(2)}) copy-start(f32[256]{0:T(256)} %param.18) | copy-start | bytes 3076
  109.4 34.4 %all-to-all-start.1 = ((f32[64,4,128]{2,1,0:T(4,128)}), f32[64,4,128]{2,1,0:T(4,128)S(1)}, u32[]{:S(2)}, u32[]{:S(2)}) async-start(f32[64,4,128]{2,1,0:T(4,128)} %get-tuple-element.21), calls=%async_computation.1 | async-start | bytes 262144 | tf_op jit(solution)/shard_map/all_to_all | solution.py:329
  125.0 12.2 %collective-permute-start = (bf16[16,48,256]{2,1,0:T(8,128)(2,1)S(1)}, bf16[16,48,256]{2,1,0:T(8,128)(2,1)S(1)}, u32[]{:S(2)}, u32[]{:S(2)}) collective-permute-start(bf16[16,48,256]{2,1,0:T(8,128)(2,1)S(1)} %get-tuple-element.18.refs_0_), channel_id=1, source_target_pairs={{0,1},{1,0},{2,3},{3,2},{4,5},{5,4},{6,7},{7,6},{8,9},{9,8},{10,11... | collective-permute-start | bytes 1179656 | tf_op jit(solution)/shard_map/ppermute | solution.py:317
  128.3 12.2 %collective-permute-start.1 = (bf16[16,48,256]{2,1,0:T(8,128)(2,1)S(1)}, bf16[16,48,256]{2,1,0:T(8,128)(2,1)S(1)}, u32[]{:S(2)}, u32[]{:S(2)}) collective-permute-start(bf16[16,48,256]{2,1,0:T(8,128)(2,1)S(1)} %get-tuple-element.18.refs_0_), channel_id=1, source_target_pairs={{0,512},{512,0},{1,513},{513,1},{2,514},{514,2},{3,515},{515,3},{4... | collective-permute-start | bytes 1179656 | tf_op jit(solution)/shard_map/ppermute | solution.py:318
  137.3 4.4 %collective-permute-start.2 = (bf16[16,48,256]{2,1,0:T(8,128)(2,1)S(1)}, bf16[16,48,256]{2,1,0:T(8,128)(2,1)S(1)}, u32[]{:S(2)}, u32[]{:S(2)}) collective-permute-start(bf16[16,48,256]{2,1,0:T(8,128)(2,1)S(1)} %collective-permute-done.refs_1_), channel_id=1, source_target_pairs={{0,512},{512,0},{1,513},{513,1},{2,514},{514,2},{3,515},{515,3},{4... | collective-permute-start | bytes 1179656 | tf_op jit(solution)/shard_map/ppermute | solution.py:319
where the time goes:
time: 145 us; the launch traced here: 144 us
  starting transfers between devices  55 us (38%)
  blocking collectives  31.2 us (22%)
  local copies, waits for them, and re-layouts  18.7 us (13%)
  waiting for transfers between devices  17.2 us (12%)
  matrix products  9.78 us (7%)
  Pallas kernels  7.09 us (5%)
  other arithmetic  4.52 us (3%)
    all_gather x1, blocking collectives, on_device(): lax.all_gather(sent, 'tensor', axis=0, tiled=True, axis_index_groups=far_...  31.2 us
    all_to_all x1, starting transfers between devices, on_device(): lax.all_to_all(packed, ALL, split_axis=0, concat_axis=0, tiled=True)  30.5 us
    all_to_all x1, starting transfers between devices, on_device(): lax.all_to_all(spread, ('half', 'dp', 'tensor'), split_axis=0, concat_axi...  15.7 us
    all_to_all x1, waiting for transfers between devices, on_device(): lax.all_to_all(packed, ALL, split_axis=0, concat_axis=0, tiled=True)  9.5 us
    unnamed x29, local copies, waits for them, and re-layouts  9.44 us
    ppermute x1, waiting for transfers between devices, on_device(): near = lax.ppermute(far, 'tensor', swap)  6.48 us
    dot_general x2, matrix products, encode_user(): jnp.einsum('hql,lhd->qhd', attention, value_heads, preferred_element_type...  4.75 us
    dot_general x2, matrix products, key_rows(): raw_keys = jnp.dot(history_rows, key_weight, preferred_element_type=F32)  4.19 us
  transfers between devices with their start and end apart: 5, of which 3 were waited for; matrix products, arithmetic and copies ran while one was open for 20% of the time, Pallas kernels for 2%

commit v1 on v0

v1 whole, which is shorter than its diff:
```python
import functools
import math

import jax
import jax.numpy as jnp
from jax import lax
from jax.experimental import pallas as pl
from jax.experimental.pallas import tpu as pltpu
from jax.sharding import PartitionSpec as P

HEADS = 8
EMB = 256
RANK = 12
STATE = 2 * RANK
SIDE = 2 * EMB
PACKED = 2 * EMB + 128
NEAR = 4
PAIR = 2
MEMBERS = 4
ALL = ("half", "tensor")
F32 = jnp.float32
BF16 = jnp.bfloat16


def encode_kernel(lengths_ref, history_ref, query_ref, weight_ref, gain_ref, interest_gain_ref, out_ref, left, right):
    seq_len, model_width = history_ref.shape
    head_dim = model_width // HEADS
    raw_keys = jnp.dot(history_ref[...], weight_ref[...], preferred_element_type=F32)
    length = lengths_ref[0, pl.program_id(0)]
    live = lax.broadcasted_iota(jnp.int32, (query_ref.shape[0], seq_len), 1) < length
    pooled = []
    for head in range(HEADS):
        lanes = slice(head * head_dim, (head + 1) * head_dim)
        raw = raw_keys[:, lanes]
        shrink = lax.rsqrt(jnp.mean(raw * raw, axis=-1, keepdims=True) + 1e-06)
        keys = (raw * shrink * gain_ref[:, lanes]).astype(BF16)
        scores = lax.dot_general(
            query_ref[:, lanes], keys, (((1,), (1,)), ((), ())), preferred_element_type=F32
        ) / math.sqrt(head_dim)
        scores = jnp.where(live, scores, -1e30)
        expo = jnp.exp(scores - jnp.max(scores, axis=-1, keepdims=True))
        attention = (expo / jnp.sum(expo, axis=-1, keepdims=True)).astype(BF16)
        pooled.append(jnp.dot(attention, history_ref[:, lanes], preferred_element_type=F32))
    heads_each = EMB // head_dim
    count = HEADS // heads_each
    for c in range(count):
        piece = jnp.concatenate(pooled[c * heads_each : (c + 1) * heads_each], axis=1)
        norm_inv = lax.rsqrt(jnp.mean(piece * piece, axis=-1, keepdims=True) + 1e-06)
        normed = piece * norm_inv * interest_gain_ref[...]
        rows = pl.ds(c, query_ref.shape[0], stride=count)
        left[rows, :] = normed[:, : EMB // 2]
        right[rows, :] = normed[:, EMB // 2 :]
    out_ref[...] = jnp.concatenate([left[...], right[...]], axis=1).astype(BF16)


def encode_users(history, queries, lengths, key_weight, key_gain, interest_gain):
    _, users, seq_len, model_width = history.shape
    query_count = queries.shape[2]
    rows = query_count * model_width // EMB

    def per_user(height, width):
        return pl.BlockSpec((None, None, height, width), lambda user: (0, user, 0, 0))

    def shared(height, width):
        return pl.BlockSpec((height, width), lambda user: (0, 0))

    return pl.pallas_call(
        encode_kernel,
        out_shape=jax.ShapeDtypeStruct((users, rows, EMB), BF16),
        grid=(users,),
        in_specs=[
            pl.BlockSpec(memory_space=pltpu.SMEM),
            per_user(seq_len, model_width),
            per_user(query_count, model_width),
            shared(model_width, model_width),
            shared(1, model_width),
            shared(1, EMB),
        ],
        out_specs=pl.BlockSpec((None, rows, EMB), lambda user: (user, 0, 0)),
        scratch_shapes=[pltpu.VMEM((rows, EMB // 2), F32)] * 2,
        compiler_params=pltpu.CompilerParams(vmem_limit_bytes=48 * 2**20),
        name="encode_users",
    )(lengths, history, queries, key_weight, key_gain[None], interest_gain[None])


def pack_kernel(rows_ref, *refs):
    inputs, (out_ref, scratch), (held, arrived) = refs[:6], refs[6:8], (refs[8:14], refs[14])
    copies = [
        pltpu.make_async_copy(source, target, arrived.at[i])
        for i, (source, target) in enumerate(zip(inputs, held))
    ]
    for copy in copies:
        copy.start()
    for copy in copies:
        copy.wait()
    wanted_ref, sparse_ref, cot_int_ref, cot_spa_ref, proj_int_ref, proj_spa_ref = held
    devices, width = out_ref.shape[0], sparse_ref.shape[1]
    batch = sparse_ref.shape[0]
    for user in range(2 * devices):
        lanes = slice((user % 2) * EMB, (user % 2 + 1) * EMB)
        out_ref[user // 2, :, lanes] = sparse_ref[rows_ref[0, user]]
    row_of = lax.broadcasted_iota(jnp.int32, (batch, batch), 0)
    pick = (row_of == wanted_ref[...]).astype(BF16)
    for j in range(width):
        cots = jnp.concatenate([cot_int_ref[:, j, :], cot_spa_ref[:, j, :]], axis=0)
        scratch[:, :STATE] = lax.dot_general(
            pick, cots, (((0,), (1,)), ((), ())), preferred_element_type=F32
        )
        proj = jnp.concatenate([proj_int_ref[j : j + 1, :], proj_spa_ref[j : j + 1, :]], axis=1)
        parts = [scratch[pl.ds(slot, devices, stride=2), :STATE] for slot in range(2)]
        parts.append(jnp.broadcast_to(proj.astype(F32), (devices, STATE)))
        parts.append(jnp.zeros((devices, 128 - 3 * STATE), F32))
        out_ref[:, j, SIDE:] = jnp.concatenate(parts, axis=1).astype(BF16)


def pack(assignment, sparse_embed, cots, projs):
    batch, width, _ = sparse_embed.shape
    inputs = [
        pltpu.with_memory_space_constraint(array, pltpu.HBM)
        for array in (assignment, sparse_embed, *cots, *projs)
    ]
    return pl.pallas_call(
        pack_kernel,
        out_shape=jax.ShapeDtypeStruct((batch // 2, width, PACKED), BF16),
        in_specs=[pl.BlockSpec(memory_space=pltpu.SMEM)]
        + [pl.BlockSpec(memory_space=pltpu.HBM)] * len(inputs),
        out_specs=pl.BlockSpec(memory_space=pltpu.VMEM),
        scratch_shapes=[pltpu.VMEM((batch, 128), F32)]
        + [pltpu.VMEM(array.shape, array.dtype) for array in inputs]
        + [pltpu.SemaphoreType.DMA((len(inputs),))],
        compiler_params=pltpu.CompilerParams(vmem_limit_bytes=32 * 2**20),
        name="pack_rows",
    )(assignment, *inputs)


def state_kernel(factor, packed_ref, interest_ref, sent_ref):
    contract_rows = (((0,), (0,)), ((), ()))
    contract_lanes = (((1,), (1,)), ((), ()))
    side = packed_ref[:, SIDE:]
    proj = side[:, 2 * STATE : 3 * STATE]
    total_int, total_spa = None, None
    for slot in range(2):
        interest = interest_ref[slot]
        sparse = packed_ref[:, slot * EMB : (slot + 1) * EMB]
        cot = side[:, slot * STATE : (slot + 1) * STATE]
        left_int = jnp.concatenate([proj[:, :RANK], cot[:, :RANK]], axis=1)
        left_spa = jnp.concatenate([proj[:, RANK:], cot[:, RANK:]], axis=1)
        summed = lax.dot_general(
            left_int, interest, contract_rows, preferred_element_type=F32
        ) + lax.dot_general(left_spa, sparse, contract_rows, preferred_element_type=F32)
        is_state = lax.broadcasted_iota(jnp.int32, summed.shape, 0) < RANK
        rounded = jnp.where(is_state, summed, summed * factor).astype(BF16)
        sent_ref[slot] = rounded
        grad = rounded[RANK:, :]
        part_int = lax.dot_general(grad, interest, contract_lanes, preferred_element_type=F32)
        part_spa = lax.dot_general(grad, sparse, contract_lanes, preferred_element_type=F32)
        total_int = part_int if total_int is None else total_int + part_int
        total_spa = part_spa if total_spa is None else total_spa + part_spa
    sent_ref[2] = jnp.concatenate([total_int, total_spa], axis=0).astype(BF16)


def make_state(packed, interest):
    vmem = pl.BlockSpec(memory_space=pltpu.VMEM)
    return pl.pallas_call(
        functools.partial(state_kernel, 1.0 / math.sqrt(EMB)),
        out_shape=jax.ShapeDtypeStruct((3, STATE, EMB), BF16),
        in_specs=[vmem, vmem],
        out_specs=vmem,
        compiler_params=pltpu.CompilerParams(vmem_limit_bytes=32 * 2**20),
        name="make_state",
    )(packed, interest)


def columns_kernel(factor, wanted_ref, cot_int_ref, cot_spa_ref, proj_int_ref, proj_spa_ref, out_ref, rows):
    users, width = wanted_ref.shape[1], proj_int_ref.shape[0]
    row_of = lax.broadcasted_iota(jnp.int32, (users, users), 0)
    pick = (row_of == wanted_ref[...]).astype(BF16)
    for kind, (cot_ref, proj_ref) in enumerate(
        ((cot_int_ref, proj_int_ref), (cot_spa_ref, proj_spa_ref))
    ):
        for j in range(width):
            cot = lax.dot_general(
                pick, cot_ref[:, j, :], (((0,), (1,)), ((), ())), preferred_element_type=F32
            )
            proj = jnp.broadcast_to(proj_ref[j : j + 1, :].astype(F32), (users, RANK))
            row = [cot * factor, proj, jnp.zeros((users, 128 - STATE), F32)]
            rows[pl.ds(kind * width + j, users, stride=8), :] = jnp.concatenate(row, axis=1)
    height = out_ref.shape[2]
    for member in range(out_ref.shape[0]):
        turned = jnp.transpose(rows[member * height : (member + 1) * height, :])
        out_ref[member] = turned[:STATE, :].astype(BF16)


def left_columns(wanted, cots, projs, factor):
    vmem = pl.BlockSpec(memory_space=pltpu.VMEM)
    users = wanted.shape[1]
    return pl.pallas_call(
        functools.partial(columns_kernel, factor),
        out_shape=jax.ShapeDtypeStruct((MEMBERS, STATE, users * 8 // MEMBERS), BF16),
        in_specs=[vmem] * 5,
        out_specs=vmem,
        scratch_shapes=[pltpu.VMEM((users * 8, 128), F32)],
        compiler_params=pltpu.CompilerParams(vmem_limit_bytes=32 * 2**20),
        name="left_columns",
    )(wanted, *cots, *projs)


def left_kernel(*refs):
    columns, left_ref = refs[:-1], refs[-1]
    blocks, height, depth = left_ref.shape[1:]
    same = lax.broadcasted_iota(jnp.int32, (STATE, STATE), 0) == lax.broadcasted_iota(
        jnp.int32, (STATE, STATE), 1
    )
    repeat = jnp.concatenate([same.astype(BF16)] * (depth // STATE), axis=1)
    owner = lax.broadcasted_iota(jnp.int32, (height, STATE), 0) // 8
    mask = jnp.concatenate([(owner == i).astype(F32) for i in range(depth // STATE)], axis=1)
    for member, column_ref in enumerate(columns):
        wide = lax.dot_general(
            column_ref[...], repeat, (((0,), (0,)), ((), ())), preferred_element_type=F32
        )
        for block in range(blocks):
            part = wide[block * height : (block + 1) * height, :]
            left_ref[member, block] = (part * mask).astype(BF16)


def left_blocks(columns):
    vmem = pl.BlockSpec(memory_space=pltpu.VMEM)
    per_block = 2 * NEAR
    height = per_block * 8
    blocks = columns[0].shape[1] // height
    return pl.pallas_call(
        left_kernel,
        out_shape=jax.ShapeDtypeStruct((len(columns), blocks, height, per_block * STATE), BF16),
        in_specs=[vmem] * len(columns),
        out_specs=vmem,
        compiler_params=pltpu.CompilerParams(vmem_limit_bytes=32 * 2**20),
        name="left_blocks",
    )(*columns)


def embed_kernel(shards, place_ref, left_ref, got_ref, *refs):
    outs, spread_ref, states = refs[:MEMBERS], refs[MEMBERS], refs[MEMBERS + 1]
    total = None
    for source in range(states.shape[0]):
        for slot in range(2):
            states[source, slot * STATE : (slot + 1) * STATE, :] = got_ref[3 * source + slot]
        part = got_ref[3 * source + 2].astype(F32)
        total = part if total is None else total + part
    total = jnp.concatenate([total, jnp.zeros((128 - STATE, total.shape[1]), F32)], axis=0)
    width = spread_ref.shape[1]
    halves = 2
    columns = total.shape[1] // halves
    for half in range(halves):
        mine = pltpu.roll(
            total[:, half * columns : (half + 1) * columns],
            columns - place_ref[0] * PAIR * width,
            1,
        )
        turned = jnp.transpose(mine)
        for member in range(PAIR):
            row = turned[member * width : (member + 1) * width, :]
            for shard in range(shards):
                spread_ref[(half * shards + shard) * PAIR + member] = row
    for block in range(left_ref.shape[1]):
        right = states[block * NEAR : (block + 1) * NEAR].reshape(NEAR * 2 * STATE, EMB)
        for member, out_ref in enumerate(outs):
            got = jnp.dot(left_ref[member, block], right, preferred_element_type=F32)
            for i in range(2 * NEAR):
                out_ref[block * 2 * NEAR + i] = got[8 * i : 8 * i + 8, :].astype(BF16)


def embed_rows(place, left, gathered, shards, width):
    vmem = pl.BlockSpec(memory_space=pltpu.VMEM)
    sources, emb = gathered.shape[0] // 3, gathered.shape[2]
    out = jax.ShapeDtypeStruct((2 * sources, 8, emb), BF16)
    return pl.pallas_call(
        functools.partial(embed_kernel, shards),
        out_shape=(out,) * MEMBERS
        + (jax.ShapeDtypeStruct((2 * shards * PAIR, width, 128), F32),),
        in_specs=[pl.BlockSpec(memory_space=pltpu.SMEM), vmem, vmem],
        out_specs=(vmem,) * (MEMBERS + 1),
        scratch_shapes=[pltpu.VMEM((sources, 2 * STATE, emb), BF16)],
        compiler_params=pltpu.CompilerParams(vmem_limit_bytes=32 * 2**20),
        name="embed_rows",
    )(place, left, gathered)


def scatter_kernel(rows_ref, *refs):
    sources, (int_ref, spa_ref) = refs[:-2], refs[-2:]
    width = int_ref.shape[1]
    for member, source in enumerate(sources):
        users = source.shape[0]
        for user in range(users):
            row = rows_ref[member * users + user]
            both = source[user].astype(F32)
            int_ref[row] = both[:width, :].astype(BF16)
            spa_ref[row] = both[width:, :].astype(BF16)


def scatter_rows(rows, sources, width):
    vmem = pl.BlockSpec(memory_space=pltpu.VMEM)
    out = jax.ShapeDtypeStruct((rows.shape[0], width, EMB), BF16)
    return pl.pallas_call(
        scatter_kernel,
        out_shape=(out, out),
        in_specs=[pl.BlockSpec(memory_space=pltpu.SMEM)] + [vmem] * len(sources),
        out_specs=(vmem, vmem),
        compiler_params=pltpu.CompilerParams(vmem_limit_bytes=32 * 2**20),
        name="scatter_rows",
    )(rows, *sources)


def on_device(
    history,
    queries,
    lengths,
    assignment,
    key_weight,
    key_gain,
    interest_gain,
    sparse_embed,
    proj_interest,
    proj_sparse,
    cot_interest,
    cot_sparse,
):
    batch_rows = assignment[0]
    batch_local, width, _ = sparse_embed.shape
    devices = batch_local // 2
    tensor = lax.axis_size("tensor")
    halves = lax.axis_size("half")
    factor = 1.0 / math.sqrt(EMB)

    cots = [cot_interest.transpose(2, 1, 0), cot_sparse.transpose(2, 1, 0)]
    packed = pack(assignment, sparse_embed, cots, [proj_interest, proj_sparse])
    arrived = lax.all_to_all(packed, ALL, split_axis=0, concat_axis=0, tiled=True)

    interest = encode_users(history, queries, lengths, key_weight, key_gain, interest_gain)

    far_count = tensor // PAIR
    far_groups = [[i + PAIR * m for m in range(far_count)] for i in range(PAIR)]
    my_half = lax.axis_index("half")
    my_tensor = lax.axis_index("tensor")
    tables = batch_rows.reshape(halves, far_count, PAIR, 2).transpose(0, 2, 1, 3)
    tables = jnp.where(my_half == 0, tables, tables[::-1])
    tables = jnp.where(my_tensor % PAIR == 0, tables, tables[:, ::-1])
    ordered_rows = tables.reshape(batch_local)
    flips = [
        [(h * tensor + z, (h ^ over_half) * tensor + (z ^ over_pair)) for h in range(halves) for z in range(tensor)]
        for over_half in range(halves)
        for over_pair in range(PAIR)
    ]
    wanted, interest = lax.optimization_barrier((ordered_rows[None], interest))
    columns = left_columns(wanted, cots, [proj_interest, proj_sparse], factor)
    left = left_blocks(
        [columns[0]] + [lax.ppermute(columns[i], ALL, flips[i]) for i in range(1, MEMBERS)]
    )
    interest, left = lax.optimization_barrier((interest, left))

    sent = make_state(arrived.reshape(devices * width, PACKED), interest)
    gathered = lax.all_gather(sent, "tensor", axis=0, tiled=True, axis_index_groups=far_groups)

    shards = lax.axis_size("dp")
    pair = my_tensor // PAIR
    *outs, spread = embed_rows(
        pair.reshape(1).astype(jnp.int32), left, gathered, shards, width
    )
    sum_groups = [
        [
            (half * shards + shard) * tensor + PAIR * m + i
            for half in range(halves)
            for shard in range(shards)
            for i in range(PAIR)
        ]
        for m in range(far_count)
    ]
    shares = lax.all_to_all(
        spread,
        ("half", "dp", "tensor"),
        split_axis=0,
        concat_axis=0,
        tiled=True,
        axis_index_groups=sum_groups,
    )
    batch_total = shards * batch_local
    proj_grads = jnp.sum(shares, axis=0)[:, :STATE] / batch_total

    crossed = {i: lax.ppermute(outs[i], ALL, flips[i]) for i in (3, 1, 2)}
    sources = [outs[0]] + [crossed[i] for i in range(1, MEMBERS)]
    grad_interest, grad_sparse = scatter_rows(ordered_rows, sources, width)
    return (grad_interest, grad_sparse, proj_grads[:, :RANK], proj_grads[:, RANK:])


def solution(mesh):
    placed = (
        P("dp", ("half", "tensor"), None, None),
        P("dp", ("half", "tensor"), None, None),
        P("dp", ("half", "tensor")),
        P("dp", None),
        P(),
        P(),
        P(),
        P("dp", ("half", "tensor"), None),
        P(("half", "tensor"), None),
        P(("half", "tensor"), None),
        P("dp", ("half", "tensor"), None),
        P("dp", ("half", "tensor"), None),
    )
    return jax.shard_map(
        on_device,
        mesh=mesh,
        in_specs=placed,
        out_specs=(
            P("dp", ("half", "tensor"), None),
            P("dp", ("half", "tensor"), None),
            P(("half", "tensor"), None),
            P(("half", "tensor"), None),
        ),
        check_vma=False,
    )
```

time: 145 us -> 141 us (0.972)
  local copies, waits for them, and re-layouts: 18.7 us -> 7.93 us
  matrix products: 9.78 us -> 0 us
  Pallas kernels: 7.09 us -> 15.3 us
  starting transfers between devices: 55 us -> 60.2 us
  waiting for transfers between devices: 17.2 us -> 22 us
  other arithmetic: 4.52 us -> 1.44 us
    dot_general x6 -> x0, matrix products: 9.78 us -> none  [the longest x2 4.75 us: encode_user(): jnp.einsum('hql,lhd->qhd', attention, value_heads, preferred_element_type...]
    pallas_call x3 -> x5, Pallas kernels: 3.66 us -> 11.9 us  [the longest x1 8.65 us: encode_users(): pl.pallas_call(encode_kernel, out_shape=jax.ShapeDtypeStruct((users, rows...]
    ppermute x3 -> x6, starting transfers between devices: 8.82 us -> 15.3 us  [the longest x3 7.72 us: on_device(): crossed = {i: lax.ppermute(outs[i], ALL, flips[i]) for i in (3, 1, 2)}]
    all_to_all x1, waiting for transfers between devices: 9.5 us -> 14.2 us  [on_device(): lax.all_to_all(packed, ALL, split_axis=0, concat_axis=0, tiled=True)]
    dot_general x1 -> x0, local copies, waits for them, and re-layouts: 3.96 us -> none  [key_rows(): raw_keys = jnp.dot(history_rows, key_weight, preferred_element_type=F32)]
    unnamed x29 -> x21, local copies, waits for them, and re-layouts: 9.44 us -> 6.68 us
    transpose x2 -> x0, local copies, waits for them, and re-layouts: 2.21 us -> none  [encode_user(): jnp.einsum('hql,lhd->qhd', attention, value_heads, preferred_element_type...]
    ppermute x3 -> x6, waiting for transfers between devices: 7.66 us -> 7.79 us  [the longest x3 4.87 us: on_device(): crossed = {i: lax.ppermute(outs[i], ALL, flips[i]) for i in (3, 1, 2)}]
  transfers between devices with their start and end apart: 5 -> 8, of which waited for: 3 -> 4; matrix products, arithmetic and copies ran while one was open for 20% -> 2% of each run, Pallas kernels for 2% -> 8%
where the time goes in v1:
time: 141 us; the launch traced here: 140 us
  starting transfers between devices  60.2 us (43%)
  blocking collectives  32.5 us (23%)
  waiting for transfers between devices  22 us (16%)
  Pallas kernels  15.3 us (11%)
  local copies, waits for them, and re-layouts  7.93 us (6%)
  other arithmetic  1.44 us (1%)
    all_gather x1, blocking collectives, on_device(): lax.all_gather(sent, 'tensor', axis=0, tiled=True, axis_index_groups=far_...  32.5 us
    all_to_all x1, starting transfers between devices, on_device(): lax.all_to_all(packed, ALL, split_axis=0, concat_axis=0, tiled=True)  30.5 us
    all_to_all x1, starting transfers between devices, on_device(): lax.all_to_all(spread, ('half', 'dp', 'tensor'), split_axis=0, concat_axi...  14.4 us
    all_to_all x1, waiting for transfers between devices, on_device(): lax.all_to_all(packed, ALL, split_axis=0, concat_axis=0, tiled=True)  14.2 us
    pallas_call x1, Pallas kernels, encode_users(): pl.pallas_call(encode_kernel, out_shape=jax.ShapeDtypeStruct((users, rows...  8.65 us
    ppermute x3, starting transfers between devices, on_device(): crossed = {i: lax.ppermute(outs[i], ALL, flips[i]) for i in (3, 1, 2)}  7.72 us
    ppermute x3, starting transfers between devices, on_device(): lax.ppermute(columns[i], ALL, flips[i])  7.59 us
    unnamed x21, local copies, waits for them, and re-layouts  6.68 us
  transfers between devices with their start and end apart: 8, of which 4 were waited for; matrix products, arithmetic and copies ran while one was open for 2% of the time, Pallas kernels for 8%

profile of v1, /device:TPU:1, one launch (start us, length us, event | category | flops | bytes accessed | tf_op | source)
XLA Modules:
  0.0 140.2 jit_solution(7666056775071767296)
XLA Ops:
  0.6 2.9 %pack_rows.1 = bf16[64,4,640]{2,1,0:T(4,128)(2,1)} custom-call(s32[1,128]{1,0:T(1,128)} %refs_0_.1, s32[1,128]{1,0:T(1,128)} %refs_0_.1, bf16[128,4,256]{2,1,0:T(4,128)(2,1)} %refs_1_.1, bf16[12,4,128]{2,1,0:T(4,128)(2,1)} %bitcast.18, bf16[12,4,128]{2,1,0:T(4,128)(2,1)} %bitcast.20, bf16[4,12]{1,0:T(4,128)(2,1)} %refs_4_.1, bf16[4,12]{1,0:T(4,128)(2,1)} %refs_5_.1), custom_call_target="tpu_custom_call" | custom-call | tf_op jit(solution)/shard_map/pack_rows/pallas_call | solution.py:122
  3.6 30.5 %all-to-all-start = ((bf16[64,4,640]{2,1,0:T(4,128)(2,1)}), bf16[64,4,640]{2,1,0:T(4,128)(2,1)S(1)}, u32[]{:S(2)}, u32[]{:S(2)}) async-start(bf16[64,4,640]{2,1,0:T(4,128)(2,1)} %pack_rows.1), calls=%async_computation | async-start | bytes 655360 | tf_op jit(solution)/shard_map/all_to_all | solution.py:336
  34.6 1.3 reduce.3
  36.4 1.6 %copy-done = bf16[1,2,512,1024]{3,2,1,0:T(8,128)(2,1)S(1)} copy-done((bf16[1,2,512,1024]{3,2,1,0:T(8,128)(2,1)S(1)}, bf16[1,2,512,1024]{3,2,1,0:T(8,128)(2,1)}, u32[]{:S(2)}) %copy-start) | copy-done | bytes 2097176
  38.0 1.6 %copy-done.1 = bf16[1024,1024]{1,0:T(8,128)(2,1)S(1)} copy-done((bf16[1024,1024]{1,0:T(8,128)(2,1)S(1)}, bf16[1024,1024]{1,0:T(8,128)(2,1)}, u32[]{:S(2)}) %copy-start.1) | copy-done | bytes 2097176
  39.6 0.9 copy-done.2
  40.5 0.7 copy-done.5
  41.2 0.7 copy-done.8
  42.5 8.7 %encode_users.1.interest_ref = bf16[2,256,256]{2,1,0:T(8,128)(2,1)S(1)} custom-call(s32[1,2]{1,0:T(1,128)S(1)} %copy-done.9, bf16[1,2,512,1024]{3,2,1,0:T(8,128)(2,1)S(1)} %copy-done, bf16[1,2,64,1024]{3,2,1,0:T(8,128)(2,1)S(1)} %copy-done.2, bf16[1024,1024]{1,0:T(8,128)(2,1)S(1)} %copy-done.1, f32[1,1024]{1,0:T(1,128)S(1)} %bitcast.22, f32[1,256]{1,0:T(1,128)S(1)} %bitcast.23), custom_call_target="tpu_custom_call" | custom-call | tf_op jit(solution)/shard_map/encode_users/pallas_call | solution.py:67
  51.6 3.4 %collective-permute-start.2 = (bf16[24,256]{1,0:T(8,128)(2,1)S(1)}, bf16[24,256]{1,0:T(8,128)(2,1)S(1)}, u32[]{:S(2)}, u32[]{:S(2)}) collective-permute-start(bf16[24,256]{1,0:T(8,128)(2,1)S(1)} %get-tuple-element.26), channel_id=1, source_target_pairs={{0,513},{1,512},{2,515},{3,514},{4,517},{5,516},{6,519},{7,518},{8... | collective-permute-start | bytes 36872 | tf_op jit(solution)/shard_map/ppermute | solution.py:356
  55.1 2.1 %collective-permute-start.1 = (bf16[24,256]{1,0:T(8,128)(2,1)S(1)}, bf16[24,256]{1,0:T(8,128)(2,1)S(1)}, u32[]{:S(2)}, u32[]{:S(2)}) collective-permute-start(bf16[24,256]{1,0:T(8,128)(2,1)S(1)} %get-tuple-element.27), channel_id=1, source_target_pairs={{0,512},{1,513},{2,514},{3,515},{4,516},{5,517},{6,518},{7,519},{8... | collective-permute-start | bytes 36872 | tf_op jit(solution)/shard_map/ppermute | solution.py:356
  57.2 2.0 %collective-permute-start = (bf16[24,256]{1,0:T(8,128)(2,1)S(1)}, bf16[24,256]{1,0:T(8,128)(2,1)S(1)}, u32[]{:S(2)}, u32[]{:S(2)}) collective-permute-start(bf16[24,256]{1,0:T(8,128)(2,1)S(1)} %get-tuple-element.28), channel_id=1, source_target_pairs={{0,1},{1,0},{2,3},{3,2},{4,5},{5,4},{6,7},{7,6},{8,9},{9,8},{10,11... | collective-permute-start | bytes 36872 | tf_op jit(solution)/shard_map/ppermute | solution.py:356
  59.3 1.4 collective-permute-done.2.refs_3_
  60.7 1.5 %collective-permute-done.refs_1_ = bf16[24,256]{1,0:T(8,128)(2,1)S(1)} collective-permute-done((bf16[24,256]{1,0:T(8,128)(2,1)S(1)}, bf16[24,256]{1,0:T(8,128)(2,1)S(1)}, u32[]{:S(2)}, u32[]{:S(2)}) %collective-permute-start) | collective-permute-done | bytes 12320 | tf_op jit(solution)/shard_map/ppermute | solution.py:356
  62.6 14.2 %all-to-all-done = bf16[64,4,640]{2,1,0:T(4,128)(2,1)S(1)} async-done(((bf16[64,4,640]{2,1,0:T(4,128)(2,1)}), bf16[64,4,640]{2,1,0:T(4,128)(2,1)S(1)}, u32[]{:S(2)}, u32[]{:S(2)}) %all-to-all-start) | async-done | bytes 327712 | tf_op jit(solution)/shard_map/all_to_all | solution.py:336
  77.4 32.5 %all_gather.3.got_ref = bf16[48,24,256]{2,1,0:T(8,128)(2,1)S(1)} all-gather(bf16[3,24,256]{2,1,0:T(8,128)(2,1)S(1)} %make_state.1), channel_id=1, replica_groups={{0,2,4,6,8,10,12,14,16,18,20,22,24,26,28,30},{1,3,5,7,9,11,13,15,17,19,..., dimensions={0}, use_global_device_ids=true | all-gather | bytes 626688 | tf_op jit(solution)/shard_map/all_gather | solution.py:361
  109.8 1.0 embed_rows.1
  110.8 14.4 %all-to-all-start.1 = ((f32[64,4,128]{2,1,0:T(4,128)}), f32[64,4,128]{2,1,0:T(4,128)S(1)}, u32[]{:S(2)}, u32[]{:S(2)}) async-start(f32[64,4,128]{2,1,0:T(4,128)} %get-tuple-element.25), calls=%async_computation.1 | async-start | bytes 262144 | tf_op jit(solution)/shard_map/all_to_all | solution.py:377
  125.2 3.3 %collective-permute-start.3 = (bf16[32,8,256]{2,1,0:T(8,128)(2,1)S(1)}, bf16[32,8,256]{2,1,0:T(8,128)(2,1)S(1)}, u32[]{:S(2)}, u32[]{:S(2)}) collective-permute-start(bf16[32,8,256]{2,1,0:T(8,128)(2,1)S(1)} %get-tuple-element.20), channel_id=1, source_target_pairs={{0,1},{1,0},{2,3},{3,2},{4,5},{5,4},{6,7},{7,6},{8,9},{9,8},{10,11... | collective-permute-start | bytes 393224 | tf_op jit(solution)/shard_map/ppermute | solution.py:388
  128.5 2.5 %collective-permute-start.4 = (bf16[32,8,256]{2,1,0:T(8,128)(2,1)S(1)}, bf16[32,8,256]{2,1,0:T(8,128)(2,1)S(1)}, u32[]{:S(2)}, u32[]{:S(2)}) collective-permute-start(bf16[32,8,256]{2,1,0:T(8,128)(2,1)S(1)} %get-tuple-element.21), channel_id=1, source_target_pairs={{0,512},{1,513},{2,514},{3,515},{4,516},{5,517},{6,518},{7,519},{8... | collective-permute-start | bytes 393224 | tf_op jit(solution)/shard_map/ppermute | solution.py:388
  131.0 2.0 %collective-permute-start.5 = (bf16[32,8,256]{2,1,0:T(8,128)(2,1)S(1)}, bf16[32,8,256]{2,1,0:T(8,128)(2,1)S(1)}, u32[]{:S(2)}, u32[]{:S(2)}) collective-permute-start(bf16[32,8,256]{2,1,0:T(8,128)(2,1)S(1)} %get-tuple-element.22), channel_id=1, source_target_pairs={{0,513},{1,512},{2,515},{3,514},{4,517},{5,516},{6,519},{7,518},{8... | collective-permute-start | bytes 393224 | tf_op jit(solution)/shard_map/ppermute | solution.py:388
  133.2 4.9 %collective-permute-done.5.refs_3_ = bf16[32,8,256]{2,1,0:T(8,128)(2,1)S(1)} collective-permute-done((bf16[32,8,256]{2,1,0:T(8,128)(2,1)S(1)}, bf16[32,8,256]{2,1,0:T(8,128)(2,1)S(1)}, u32[]{:S(2)}, u32[]{:S(2)}) %collective-permute-start.5) | collective-permute-done | bytes 131104 | tf_op jit(solution)/shard_map/ppermute | solution.py:388
  138.0 1.5 %scatter_rows.1 = (bf16[128,4,256]{2,1,0:T(4,128)(2,1)}, bf16[128,4,256]{2,1,0:T(4,128)(2,1)}) custom-call(s32[128]{0:T(128)S(1)} %reshape.17.rows_ref, bf16[32,8,256]{2,1,0:T(8,128)(2,1)S(1)} %get-tuple-element.19.refs_0_, bf16[32,8,256]{2,1,0:T(8,128)(2,1)S(1)} %collective-permute-done.3.refs_1_, bf16[32,8,256]{2,1,0:T(8,128)(2,1)S(1)} %collective-permute-done.4.refs_2_, ...), custom_call_target="tpu_custom_call" | custom-call | tf_op jit(solution)/shard_map/scatter_rows/pallas_call | solution.py:303
  139.6 0.7 fusion
  (34 shorter events, 3.2 us)
Async XLA Ops:
  3.6 73.2 %all-to-all-start = ((bf16[64,4,640]{2,1,0:T(4,128)(2,1)}), bf16[64,4,640]{2,1,0:T(4,128)(2,1)S(1)}, u32[]{:S(2)}, u32[]{:S(2)}) async-start(bf16[64,4,640]{2,1,0:T(4,128)(2,1)} %pack_rows.1), calls=%async_computation | async-start | bytes 655360 | tf_op jit(solution)/shard_map/all_to_all | solution.py:336
  36.4 1.6 %copy-start = (bf16[1,2,512,1024]{3,2,1,0:T(8,128)(2,1)S(1)}, bf16[1,2,512,1024]{3,2,1,0:T(8,128)(2,1)}, u32[]{:S(2)}) copy-start(bf16[1,2,512,1024]{3,2,1,0:T(8,128)(2,1)} %history_ref.1) | copy-start | bytes 6291460
  38.0 1.6 %copy-start.1 = (bf16[1024,1024]{1,0:T(8,128)(2,1)S(1)}, bf16[1024,1024]{1,0:T(8,128)(2,1)}, u32[]{:S(2)}) copy-start(bf16[1024,1024]{1,0:T(8,128)(2,1)} %weight_ref.1) | copy-start | bytes 6291460
  39.6 0.9 copy-start.2
  40.5 0.7 copy-start.5
  41.2 0.7 copy-start.8
  41.9 0.7 copy-start.9
  42.5 8.7 %copy-start.3 = (bf16[128,4,12]{0,1,2:T(4,128)(2,1)S(1)}, bf16[128,4,12]{0,1,2:T(4,128)(2,1)}, u32[]{:S(2)}) copy-start(bf16[128,4,12]{0,1,2:T(4,128)(2,1)} %param.22) | copy-start | bytes 36868
  42.5 8.7 %copy-start.4 = (bf16[128,4,12]{0,1,2:T(4,128)(2,1)S(1)}, bf16[128,4,12]{0,1,2:T(4,128)(2,1)}, u32[]{:S(2)}) copy-start(bf16[128,4,12]{0,1,2:T(4,128)(2,1)} %param.23) | copy-start | bytes 36868
  42.5 8.7 %copy-start.6 = (bf16[4,12]{1,0:T(4,128)(2,1)S(1)}, bf16[4,12]{1,0:T(4,128)(2,1)}, u32[]{:S(2)}) copy-start(bf16[4,12]{1,0:T(4,128)(2,1)} %refs_4_.1) | copy-start | bytes 292
  42.5 8.7 %copy-start.7 = (bf16[4,12]{1,0:T(4,128)(2,1)S(1)}, bf16[4,12]{1,0:T(4,128)(2,1)}, u32[]{:S(2)}) copy-start(bf16[4,12]{1,0:T(4,128)(2,1)} %refs_5_.1) | copy-start | bytes 292
  51.6 9.0 %collective-permute-start.2 = (bf16[24,256]{1,0:T(8,128)(2,1)S(1)}, bf16[24,256]{1,0:T(8,128)(2,1)S(1)}, u32[]{:S(2)}, u32[]{:S(2)}) collective-permute-start(bf16[24,256]{1,0:T(8,128)(2,1)S(1)} %get-tuple-element.26), channel_id=1, source_target_pairs={{0,513},{1,512},{2,515},{3,514},{4,517},{5,516},{6,519},{7,518},{8... | collective-permute-start | bytes 36872 | tf_op jit(solution)/shard_map/ppermute | solution.py:356
  55.1 5.6 %collective-permute-start.1 = (bf16[24,256]{1,0:T(8,128)(2,1)S(1)}, bf16[24,256]{1,0:T(8,128)(2,1)S(1)}, u32[]{:S(2)}, u32[]{:S(2)}) collective-permute-start(bf16[24,256]{1,0:T(8,128)(2,1)S(1)} %get-tuple-element.27), channel_id=1, source_target_pairs={{0,512},{1,513},{2,514},{3,515},{4,516},{5,517},{6,518},{7,519},{8... | collective-permute-start | bytes 36872 | tf_op jit(solution)/shard_map/ppermute | solution.py:356
  57.2 5.0 %collective-permute-start = (bf16[24,256]{1,0:T(8,128)(2,1)S(1)}, bf16[24,256]{1,0:T(8,128)(2,1)S(1)}, u32[]{:S(2)}, u32[]{:S(2)}) collective-permute-start(bf16[24,256]{1,0:T(8,128)(2,1)S(1)} %get-tuple-element.28), channel_id=1, source_target_pairs={{0,1},{1,0},{2,3},{3,2},{4,5},{5,4},{6,7},{7,6},{8,9},{9,8},{10,11... | collective-permute-start | bytes 36872 | tf_op jit(solution)/shard_map/ppermute | solution.py:356
  110.8 28.6 %all-to-all-start.1 = ((f32[64,4,128]{2,1,0:T(4,128)}), f32[64,4,128]{2,1,0:T(4,128)S(1)}, u32[]{:S(2)}, u32[]{:S(2)}) async-start(f32[64,4,128]{2,1,0:T(4,128)} %get-tuple-element.25), calls=%async_computation.1 | async-start | bytes 262144 | tf_op jit(solution)/shard_map/all_to_all | solution.py:377
  125.2 7.9 %collective-permute-start.3 = (bf16[32,8,256]{2,1,0:T(8,128)(2,1)S(1)}, bf16[32,8,256]{2,1,0:T(8,128)(2,1)S(1)}, u32[]{:S(2)}, u32[]{:S(2)}) collective-permute-start(bf16[32,8,256]{2,1,0:T(8,128)(2,1)S(1)} %get-tuple-element.20), channel_id=1, source_target_pairs={{0,1},{1,0},{2,3},{3,2},{4,5},{5,4},{6,7},{7,6},{8,9},{9,8},{10,11... | collective-permute-start | bytes 393224 | tf_op jit(solution)/shard_map/ppermute | solution.py:388
  128.5 4.6 %collective-permute-start.4 = (bf16[32,8,256]{2,1,0:T(8,128)(2,1)S(1)}, bf16[32,8,256]{2,1,0:T(8,128)(2,1)S(1)}, u32[]{:S(2)}, u32[]{:S(2)}) collective-permute-start(bf16[32,8,256]{2,1,0:T(8,128)(2,1)S(1)} %get-tuple-element.21), channel_id=1, source_target_pairs={{0,512},{1,513},{2,514},{3,515},{4,516},{5,517},{6,518},{7,519},{8... | collective-permute-start | bytes 393224 | tf_op jit(solution)/shard_map/ppermute | solution.py:388
  131.0 7.0 %collective-permute-start.5 = (bf16[32,8,256]{2,1,0:T(8,128)(2,1)S(1)}, bf16[32,8,256]{2,1,0:T(8,128)(2,1)S(1)}, u32[]{:S(2)}, u32[]{:S(2)}) collective-permute-start(bf16[32,8,256]{2,1,0:T(8,128)(2,1)S(1)} %get-tuple-element.22), channel_id=1, source_target_pairs={{0,513},{1,512},{2,515},{3,514},{4,517},{5,516},{6,519},{7,518},{8... | collective-permute-start | bytes 393224 | tf_op jit(solution)/shard_map/ppermute | solution.py:388

commit v2 on v1

--- a/solution.py
+++ b/solution.py
@@ -385,9 +385,11 @@
     batch_total = shards * batch_local
     proj_grads = jnp.sum(shares, axis=0)[:, :STATE] / batch_total
 
-    crossed = {i: lax.ppermute(outs[i], ALL, flips[i]) for i in (3, 1, 2)}
-    sources = [outs[0]] + [crossed[i] for i in range(1, MEMBERS)]
-    grad_interest, grad_sparse = scatter_rows(ordered_rows, sources, width)
+    sent_order = [3, 1, 2]
+    sources = [outs[0]] + [lax.ppermute(outs[i], ALL, flips[i]) for i in sent_order]
+    by_member = ordered_rows.reshape(MEMBERS, batch_local // MEMBERS)
+    sent_rows = jnp.stack([by_member[i] for i in [0] + sent_order]).reshape(batch_local)
+    grad_interest, grad_sparse = scatter_rows(sent_rows, sources, width)
     return (grad_interest, grad_sparse, proj_grads[:, :RANK], proj_grads[:, RANK:])
 
 

time: 141 us -> 138 us (0.979)
  waiting for transfers between devices: 22 us -> 19.3 us
    ppermute x3, waiting for transfers between devices: 4.87 us -> 2.21 us  [on_device(): lax.ppermute(outs[i], ALL, flips[i])]
where the time goes in v2:
time: 138 us
  starting transfers between devices  60.4 us (44%)
  blocking collectives  32.5 us (24%)
  waiting for transfers between devices  19.3 us (14%)
  Pallas kernels  15.3 us (11%)
  local copies, waits for them, and re-layouts  7.98 us (6%)
  other arithmetic  1.45 us (1%)
    all_gather x1, blocking collectives, on_device(): lax.all_gather(sent, 'tensor', axis=0, tiled=True, axis_index_groups=far_...  32.5 us
    all_to_all x1, starting transfers between devices, on_device(): lax.all_to_all(packed, ALL, split_axis=0, concat_axis=0, tiled=True)  30.5 us
    all_to_all x1, starting transfers between devices, on_device(): lax.all_to_all(spread, ('half', 'dp', 'tensor'), split_axis=0, concat_axi...  14.4 us
    all_to_all x1, waiting for transfers between devices, on_device(): lax.all_to_all(packed, ALL, split_axis=0, concat_axis=0, tiled=True)  14.2 us
    pallas_call x1, Pallas kernels, encode_users(): pl.pallas_call(encode_kernel, out_shape=jax.ShapeDtypeStruct((users, rows...  8.65 us
    ppermute x3, starting transfers between devices, on_device(): lax.ppermute(outs[i], ALL, flips[i])  7.86 us
    ppermute x3, starting transfers between devices, on_device(): lax.ppermute(columns[i], ALL, flips[i])  7.59 us
    unnamed x21, local copies, waits for them, and re-layouts  6.68 us
  transfers between devices with their start and end apart: 8, of which 4 were waited for; matrix products, arithmetic and copies ran while one was open for 2% of the time, Pallas kernels for 8%

profile of v2, /device:TPU:1, one launch (start us, length us, event | category | flops | bytes accessed | tf_op | source)
XLA Modules:
  0.0 137.8 jit_solution(123931371782410096)
XLA Ops:
  0.6 2.9 %pack_rows.1 = bf16[64,4,640]{2,1,0:T(4,128)(2,1)} custom-call(s32[1,128]{1,0:T(1,128)} %refs_0_.1, s32[1,128]{1,0:T(1,128)} %refs_0_.1, bf16[128,4,256]{2,1,0:T(4,128)(2,1)} %refs_1_.1, bf16[12,4,128]{2,1,0:T(4,128)(2,1)} %bitcast.18, bf16[12,4,128]{2,1,0:T(4,128)(2,1)} %bitcast.20, bf16[4,12]{1,0:T(4,128)(2,1)} %refs_4_.1, bf16[4,12]{1,0:T(4,128)(2,1)} %refs_5_.1), custom_call_target="tpu_custom_call" | custom-call | tf_op jit(solution)/shard_map/pack_rows/pallas_call | solution.py:122
  3.6 30.5 %all-to-all-start = ((bf16[64,4,640]{2,1,0:T(4,128)(2,1)}), bf16[64,4,640]{2,1,0:T(4,128)(2,1)S(1)}, u32[]{:S(2)}, u32[]{:S(2)}) async-start(bf16[64,4,640]{2,1,0:T(4,128)(2,1)} %pack_rows.1), calls=%async_computation | async-start | bytes 655360 | tf_op jit(solution)/shard_map/all_to_all | solution.py:336
  34.6 1.3 reduce.3
  36.4 1.6 %copy-done = bf16[1,2,512,1024]{3,2,1,0:T(8,128)(2,1)S(1)} copy-done((bf16[1,2,512,1024]{3,2,1,0:T(8,128)(2,1)S(1)}, bf16[1,2,512,1024]{3,2,1,0:T(8,128)(2,1)}, u32[]{:S(2)}) %copy-start) | copy-done | bytes 2097176
  38.0 1.6 %copy-done.1 = bf16[1024,1024]{1,0:T(8,128)(2,1)S(1)} copy-done((bf16[1024,1024]{1,0:T(8,128)(2,1)S(1)}, bf16[1024,1024]{1,0:T(8,128)(2,1)}, u32[]{:S(2)}) %copy-start.1) | copy-done | bytes 2097176
  39.6 0.9 copy-done.2
  40.5 0.7 copy-done.5
  41.2 0.7 copy-done.8
  42.5 8.6 %encode_users.1.interest_ref = bf16[2,256,256]{2,1,0:T(8,128)(2,1)S(1)} custom-call(s32[1,2]{1,0:T(1,128)S(1)} %copy-done.9, bf16[1,2,512,1024]{3,2,1,0:T(8,128)(2,1)S(1)} %copy-done, bf16[1,2,64,1024]{3,2,1,0:T(8,128)(2,1)S(1)} %copy-done.2, bf16[1024,1024]{1,0:T(8,128)(2,1)S(1)} %copy-done.1, f32[1,1024]{1,0:T(1,128)S(1)} %bitcast.22, f32[1,256]{1,0:T(1,128)S(1)} %bitcast.23), custom_call_target="tpu_custom_call" | custom-call | tf_op jit(solution)/shard_map/encode_users/pallas_call | solution.py:67
  51.6 3.4 %collective-permute-start.2 = (bf16[24,256]{1,0:T(8,128)(2,1)S(1)}, bf16[24,256]{1,0:T(8,128)(2,1)S(1)}, u32[]{:S(2)}, u32[]{:S(2)}) collective-permute-start(bf16[24,256]{1,0:T(8,128)(2,1)S(1)} %get-tuple-element.26), channel_id=1, source_target_pairs={{0,513},{1,512},{2,515},{3,514},{4,517},{5,516},{6,519},{7,518},{8... | collective-permute-start | bytes 36872 | tf_op jit(solution)/shard_map/ppermute | solution.py:356
  55.1 2.1 %collective-permute-start.1 = (bf16[24,256]{1,0:T(8,128)(2,1)S(1)}, bf16[24,256]{1,0:T(8,128)(2,1)S(1)}, u32[]{:S(2)}, u32[]{:S(2)}) collective-permute-start(bf16[24,256]{1,0:T(8,128)(2,1)S(1)} %get-tuple-element.27), channel_id=1, source_target_pairs={{0,512},{1,513},{2,514},{3,515},{4,516},{5,517},{6,518},{7,519},{8... | collective-permute-start | bytes 36872 | tf_op jit(solution)/shard_map/ppermute | solution.py:356
  57.2 2.0 %collective-permute-start = (bf16[24,256]{1,0:T(8,128)(2,1)S(1)}, bf16[24,256]{1,0:T(8,128)(2,1)S(1)}, u32[]{:S(2)}, u32[]{:S(2)}) collective-permute-start(bf16[24,256]{1,0:T(8,128)(2,1)S(1)} %get-tuple-element.28), channel_id=1, source_target_pairs={{0,1},{1,0},{2,3},{3,2},{4,5},{5,4},{6,7},{7,6},{8,9},{9,8},{10,11... | collective-permute-start | bytes 36872 | tf_op jit(solution)/shard_map/ppermute | solution.py:356
  59.3 1.4 %collective-permute-done.2.refs_3_ = bf16[24,256]{1,0:T(8,128)(2,1)S(1)} collective-permute-done((bf16[24,256]{1,0:T(8,128)(2,1)S(1)}, bf16[24,256]{1,0:T(8,128)(2,1)S(1)}, u32[]{:S(2)}, u32[]{:S(2)}) %collective-permute-start.2) | collective-permute-done | bytes 12320 | tf_op jit(solution)/shard_map/ppermute | solution.py:356
  60.7 1.5 %collective-permute-done.refs_1_ = bf16[24,256]{1,0:T(8,128)(2,1)S(1)} collective-permute-done((bf16[24,256]{1,0:T(8,128)(2,1)S(1)}, bf16[24,256]{1,0:T(8,128)(2,1)S(1)}, u32[]{:S(2)}, u32[]{:S(2)}) %collective-permute-start) | collective-permute-done | bytes 12320 | tf_op jit(solution)/shard_map/ppermute | solution.py:356
  62.6 14.2 %all-to-all-done = bf16[64,4,640]{2,1,0:T(4,128)(2,1)S(1)} async-done(((bf16[64,4,640]{2,1,0:T(4,128)(2,1)}), bf16[64,4,640]{2,1,0:T(4,128)(2,1)S(1)}, u32[]{:S(2)}, u32[]{:S(2)}) %all-to-all-start) | async-done | bytes 327712 | tf_op jit(solution)/shard_map/all_to_all | solution.py:336
  77.4 32.5 %all_gather.3.got_ref = bf16[48,24,256]{2,1,0:T(8,128)(2,1)S(1)} all-gather(bf16[3,24,256]{2,1,0:T(8,128)(2,1)S(1)} %make_state.1), channel_id=1, replica_groups={{0,2,4,6,8,10,12,14,16,18,20,22,24,26,28,30},{1,3,5,7,9,11,13,15,17,19,..., dimensions={0}, use_global_device_ids=true | all-gather | bytes 626688 | tf_op jit(solution)/shard_map/all_gather | solution.py:361
  109.8 1.0 embed_rows.1
  110.8 14.4 %all-to-all-start.1 = ((f32[64,4,128]{2,1,0:T(4,128)}), f32[64,4,128]{2,1,0:T(4,128)S(1)}, u32[]{:S(2)}, u32[]{:S(2)}) async-start(f32[64,4,128]{2,1,0:T(4,128)} %get-tuple-element.25), calls=%async_computation.1 | async-start | bytes 262144 | tf_op jit(solution)/shard_map/all_to_all | solution.py:377
  125.3 3.4 %collective-permute-start.3 = (bf16[32,8,256]{2,1,0:T(8,128)(2,1)S(1)}, bf16[32,8,256]{2,1,0:T(8,128)(2,1)S(1)}, u32[]{:S(2)}, u32[]{:S(2)}) collective-permute-start(bf16[32,8,256]{2,1,0:T(8,128)(2,1)S(1)} %get-tuple-element.20), channel_id=1, source_target_pairs={{0,513},{1,512},{2,515},{3,514},{4,517},{5,516},{6,519},{7,518},{8... | collective-permute-start | bytes 393224 | tf_op jit(solution)/shard_map/ppermute | solution.py:389
  128.8 2.1 %collective-permute-start.4 = (bf16[32,8,256]{2,1,0:T(8,128)(2,1)S(1)}, bf16[32,8,256]{2,1,0:T(8,128)(2,1)S(1)}, u32[]{:S(2)}, u32[]{:S(2)}) collective-permute-start(bf16[32,8,256]{2,1,0:T(8,128)(2,1)S(1)} %get-tuple-element.21), channel_id=1, source_target_pairs={{0,1},{1,0},{2,3},{3,2},{4,5},{5,4},{6,7},{7,6},{8,9},{9,8},{10,11... | collective-permute-start | bytes 393224 | tf_op jit(solution)/shard_map/ppermute | solution.py:389
  130.9 2.3 %collective-permute-start.5 = (bf16[32,8,256]{2,1,0:T(8,128)(2,1)S(1)}, bf16[32,8,256]{2,1,0:T(8,128)(2,1)S(1)}, u32[]{:S(2)}, u32[]{:S(2)}) collective-permute-start(bf16[32,8,256]{2,1,0:T(8,128)(2,1)S(1)} %get-tuple-element.22), channel_id=1, source_target_pairs={{0,512},{1,513},{2,514},{3,515},{4,516},{5,517},{6,518},{7,519},{8... | collective-permute-start | bytes 393224 | tf_op jit(solution)/shard_map/ppermute | solution.py:389
  133.3 2.2 %collective-permute-done.4.refs_2_ = bf16[32,8,256]{2,1,0:T(8,128)(2,1)S(1)} collective-permute-done((bf16[32,8,256]{2,1,0:T(8,128)(2,1)S(1)}, bf16[32,8,256]{2,1,0:T(8,128)(2,1)S(1)}, u32[]{:S(2)}, u32[]{:S(2)}) %collective-permute-start.4) | collective-permute-done | bytes 131104 | tf_op jit(solution)/shard_map/ppermute | solution.py:389
  135.5 1.5 %scatter_rows.1 = (bf16[128,4,256]{2,1,0:T(4,128)(2,1)}, bf16[128,4,256]{2,1,0:T(4,128)(2,1)}) custom-call(s32[128]{0:T(128)S(1)} %reshape.17.rows_ref, bf16[32,8,256]{2,1,0:T(8,128)(2,1)S(1)} %get-tuple-element.19.refs_0_, bf16[32,8,256]{2,1,0:T(8,128)(2,1)S(1)} %collective-permute-done.3.refs_1_, bf16[32,8,256]{2,1,0:T(8,128)(2,1)S(1)} %collective-permute-done.4.refs_2_, ...), custom_call_target="tpu_custom_call" | custom-call | tf_op jit(solution)/shard_map/scatter_rows/pallas_call | solution.py:303
  137.1 0.7 fusion
  (38 shorter events, 3.2 us)
Async XLA Ops:
  3.6 73.2 %all-to-all-start = ((bf16[64,4,640]{2,1,0:T(4,128)(2,1)}), bf16[64,4,640]{2,1,0:T(4,128)(2,1)S(1)}, u32[]{:S(2)}, u32[]{:S(2)}) async-start(bf16[64,4,640]{2,1,0:T(4,128)(2,1)} %pack_rows.1), calls=%async_computation | async-start | bytes 655360 | tf_op jit(solution)/shard_map/all_to_all | solution.py:336
  36.4 1.6 %copy-start = (bf16[1,2,512,1024]{3,2,1,0:T(8,128)(2,1)S(1)}, bf16[1,2,512,1024]{3,2,1,0:T(8,128)(2,1)}, u32[]{:S(2)}) copy-start(bf16[1,2,512,1024]{3,2,1,0:T(8,128)(2,1)} %history_ref.1) | copy-start | bytes 6291460
  38.0 1.6 %copy-start.1 = (bf16[1024,1024]{1,0:T(8,128)(2,1)S(1)}, bf16[1024,1024]{1,0:T(8,128)(2,1)}, u32[]{:S(2)}) copy-start(bf16[1024,1024]{1,0:T(8,128)(2,1)} %weight_ref.1) | copy-start | bytes 6291460
  39.6 0.9 copy-start.2
  40.5 0.7 copy-start.5
  41.2 0.7 copy-start.8
  41.9 0.7 copy-start.9
  42.5 8.7 %copy-start.3 = (bf16[128,4,12]{0,1,2:T(4,128)(2,1)S(1)}, bf16[128,4,12]{0,1,2:T(4,128)(2,1)}, u32[]{:S(2)}) copy-start(bf16[128,4,12]{0,1,2:T(4,128)(2,1)} %param.22) | copy-start | bytes 36868
  42.5 8.7 %copy-start.4 = (bf16[128,4,12]{0,1,2:T(4,128)(2,1)S(1)}, bf16[128,4,12]{0,1,2:T(4,128)(2,1)}, u32[]{:S(2)}) copy-start(bf16[128,4,12]{0,1,2:T(4,128)(2,1)} %param.23) | copy-start | bytes 36868
  42.5 8.7 %copy-start.6 = (bf16[4,12]{1,0:T(4,128)(2,1)S(1)}, bf16[4,12]{1,0:T(4,128)(2,1)}, u32[]{:S(2)}) copy-start(bf16[4,12]{1,0:T(4,128)(2,1)} %refs_4_.1) | copy-start | bytes 292
  42.5 8.7 %copy-start.7 = (bf16[4,12]{1,0:T(4,128)(2,1)S(1)}, bf16[4,12]{1,0:T(4,128)(2,1)}, u32[]{:S(2)}) copy-start(bf16[4,12]{1,0:T(4,128)(2,1)} %refs_5_.1) | copy-start | bytes 292
  51.6 9.0 %collective-permute-start.2 = (bf16[24,256]{1,0:T(8,128)(2,1)S(1)}, bf16[24,256]{1,0:T(8,128)(2,1)S(1)}, u32[]{:S(2)}, u32[]{:S(2)}) collective-permute-start(bf16[24,256]{1,0:T(8,128)(2,1)S(1)} %get-tuple-element.26), channel_id=1, source_target_pairs={{0,513},{1,512},{2,515},{3,514},{4,517},{5,516},{6,519},{7,518},{8... | collective-permute-start | bytes 36872 | tf_op jit(solution)/shard_map/ppermute | solution.py:356
  55.1 5.6 %collective-permute-start.1 = (bf16[24,256]{1,0:T(8,128)(2,1)S(1)}, bf16[24,256]{1,0:T(8,128)(2,1)S(1)}, u32[]{:S(2)}, u32[]{:S(2)}) collective-permute-start(bf16[24,256]{1,0:T(8,128)(2,1)S(1)} %get-tuple-element.27), channel_id=1, source_target_pairs={{0,512},{1,513},{2,514},{3,515},{4,516},{5,517},{6,518},{7,519},{8... | collective-permute-start | bytes 36872 | tf_op jit(solution)/shard_map/ppermute | solution.py:356
  57.2 5.0 %collective-permute-start = (bf16[24,256]{1,0:T(8,128)(2,1)S(1)}, bf16[24,256]{1,0:T(8,128)(2,1)S(1)}, u32[]{:S(2)}, u32[]{:S(2)}) collective-permute-start(bf16[24,256]{1,0:T(8,128)(2,1)S(1)} %get-tuple-element.28), channel_id=1, source_target_pairs={{0,1},{1,0},{2,3},{3,2},{4,5},{5,4},{6,7},{7,6},{8,9},{9,8},{10,11... | collective-permute-start | bytes 36872 | tf_op jit(solution)/shard_map/ppermute | solution.py:356
  110.8 26.2 %all-to-all-start.1 = ((f32[64,4,128]{2,1,0:T(4,128)}), f32[64,4,128]{2,1,0:T(4,128)S(1)}, u32[]{:S(2)}, u32[]{:S(2)}) async-start(f32[64,4,128]{2,1,0:T(4,128)} %get-tuple-element.25), calls=%async_computation.1 | async-start | bytes 262144 | tf_op jit(solution)/shard_map/all_to_all | solution.py:377
  125.3 8.0 %collective-permute-start.3 = (bf16[32,8,256]{2,1,0:T(8,128)(2,1)S(1)}, bf16[32,8,256]{2,1,0:T(8,128)(2,1)S(1)}, u32[]{:S(2)}, u32[]{:S(2)}) collective-permute-start(bf16[32,8,256]{2,1,0:T(8,128)(2,1)S(1)} %get-tuple-element.20), channel_id=1, source_target_pairs={{0,513},{1,512},{2,515},{3,514},{4,517},{5,516},{6,519},{7,518},{8... | collective-permute-start | bytes 393224 | tf_op jit(solution)/shard_map/ppermute | solution.py:389
  128.8 6.8 %collective-permute-start.4 = (bf16[32,8,256]{2,1,0:T(8,128)(2,1)S(1)}, bf16[32,8,256]{2,1,0:T(8,128)(2,1)S(1)}, u32[]{:S(2)}, u32[]{:S(2)}) collective-permute-start(bf16[32,8,256]{2,1,0:T(8,128)(2,1)S(1)} %get-tuple-element.21), channel_id=1, source_target_pairs={{0,1},{1,0},{2,3},{3,2},{4,5},{5,4},{6,7},{7,6},{8,9},{9,8},{10,11... | collective-permute-start | bytes 393224 | tf_op jit(solution)/shard_map/ppermute | solution.py:389
  130.9 4.7 %collective-permute-start.5 = (bf16[32,8,256]{2,1,0:T(8,128)(2,1)S(1)}, bf16[32,8,256]{2,1,0:T(8,128)(2,1)S(1)}, u32[]{:S(2)}, u32[]{:S(2)}) collective-permute-start(bf16[32,8,256]{2,1,0:T(8,128)(2,1)S(1)} %get-tuple-element.22), channel_id=1, source_target_pairs={{0,512},{1,513},{2,514},{3,515},{4,516},{5,517},{6,518},{7,519},{8... | collective-permute-start | bytes 393224 | tf_op jit(solution)/shard_map/ppermute | solution.py:389

commit v3 on v2

--- a/solution.py
+++ b/solution.py
@@ -91,14 +91,11 @@
     ]
     for copy in copies:
         copy.start()
-    for copy in copies:
-        copy.wait()
+    for i in (0, 2, 3, 4, 5):
+        copies[i].wait()
     wanted_ref, sparse_ref, cot_int_ref, cot_spa_ref, proj_int_ref, proj_spa_ref = held
     devices, width = out_ref.shape[0], sparse_ref.shape[1]
     batch = sparse_ref.shape[0]
-    for user in range(2 * devices):
-        lanes = slice((user % 2) * EMB, (user % 2 + 1) * EMB)
-        out_ref[user // 2, :, lanes] = sparse_ref[rows_ref[0, user]]
     row_of = lax.broadcasted_iota(jnp.int32, (batch, batch), 0)
     pick = (row_of == wanted_ref[...]).astype(BF16)
     for j in range(width):
@@ -111,6 +108,10 @@
         parts.append(jnp.broadcast_to(proj.astype(F32), (devices, STATE)))
         parts.append(jnp.zeros((devices, 128 - 3 * STATE), F32))
         out_ref[:, j, SIDE:] = jnp.concatenate(parts, axis=1).astype(BF16)
+    copies[1].wait()
+    for user in range(2 * devices):
+        lanes = slice((user % 2) * EMB, (user % 2 + 1) * EMB)
+        out_ref[user // 2, :, lanes] = sparse_ref[rows_ref[0, user]]
 
 
 def pack(assignment, sparse_embed, cots, projs):
@@ -266,13 +267,15 @@
         for member, out_ref in enumerate(outs):
             got = jnp.dot(left_ref[member, block], right, preferred_element_type=F32)
             for i in range(2 * NEAR):
-                out_ref[block * 2 * NEAR + i] = got[8 * i : 8 * i + 8, :].astype(BF16)
+                for kind in range(2):
+                    first = 8 * i + kind * width
+                    out_ref[block * 2 * NEAR + i, kind] = got[first : first + width, :].astype(BF16)
 
 
 def embed_rows(place, left, gathered, shards, width):
     vmem = pl.BlockSpec(memory_space=pltpu.VMEM)
     sources, emb = gathered.shape[0] // 3, gathered.shape[2]
-    out = jax.ShapeDtypeStruct((2 * sources, 8, emb), BF16)
+    out = jax.ShapeDtypeStruct((2 * sources, 2, width, emb), BF16)
     return pl.pallas_call(
         functools.partial(embed_kernel, shards),
         out_shape=(out,) * MEMBERS
@@ -287,14 +290,12 @@
 
 def scatter_kernel(rows_ref, *refs):
     sources, (int_ref, spa_ref) = refs[:-2], refs[-2:]
-    width = int_ref.shape[1]
     for member, source in enumerate(sources):
         users = source.shape[0]
         for user in range(users):
             row = rows_ref[member * users + user]
-            both = source[user].astype(F32)
-            int_ref[row] = both[:width, :].astype(BF16)
-            spa_ref[row] = both[width:, :].astype(BF16)
+            int_ref[row] = source[user, 0]
+            spa_ref[row] = source[user, 1]
 
 
 def scatter_rows(rows, sources, width):

time: 138 us -> 138 us (level)
  no operation moved by 1% of the time
where the time goes in v3:
time: 138 us
  starting transfers between devices  60.4 us (44%)
  blocking collectives  32.5 us (24%)
  waiting for transfers between devices  19.3 us (14%)
  Pallas kernels  15.2 us (11%)
  local copies, waits for them, and re-layouts  7.98 us (6%)
  other arithmetic  1.45 us (1%)
    all_gather x1, blocking collectives, on_device(): lax.all_gather(sent, 'tensor', axis=0, tiled=True, axis_index_groups=far_...  32.5 us
    all_to_all x1, starting transfers between devices, on_device(): lax.all_to_all(packed, ALL, split_axis=0, concat_axis=0, tiled=True)  30.5 us
    all_to_all x1, starting transfers between devices, on_device(): lax.all_to_all(spread, ('half', 'dp', 'tensor'), split_axis=0, concat_axi...  14.4 us
    all_to_all x1, waiting for transfers between devices, on_device(): lax.all_to_all(packed, ALL, split_axis=0, concat_axis=0, tiled=True)  14.2 us
    pallas_call x1, Pallas kernels, encode_users(): pl.pallas_call(encode_kernel, out_shape=jax.ShapeDtypeStruct((users, rows...  8.65 us
    ppermute x3, starting transfers between devices, on_device(): lax.ppermute(outs[i], ALL, flips[i])  7.86 us
    ppermute x3, starting transfers between devices, on_device(): lax.ppermute(columns[i], ALL, flips[i])  7.59 us
    unnamed x21, local copies, waits for them, and re-layouts  6.68 us
  transfers between devices with their start and end apart: 8, of which 4 were waited for; matrix products, arithmetic and copies ran while one was open for 2% of the time, Pallas kernels for 8%

profile of v3, /device:TPU:1, one launch (start us, length us, event | category | flops | bytes accessed | tf_op | source)
XLA Modules:
  0.0 137.7 jit_solution(1205094892698266924)
XLA Ops:
  0.6 2.8 %pack_rows.1 = bf16[64,4,640]{2,1,0:T(4,128)(2,1)} custom-call(s32[1,128]{1,0:T(1,128)} %refs_0_.1, s32[1,128]{1,0:T(1,128)} %refs_0_.1, bf16[128,4,256]{2,1,0:T(4,128)(2,1)} %refs_1_.1, bf16[12,4,128]{2,1,0:T(4,128)(2,1)} %bitcast.18, bf16[12,4,128]{2,1,0:T(4,128)(2,1)} %bitcast.20, bf16[4,12]{1,0:T(4,128)(2,1)} %refs_4_.1, bf16[4,12]{1,0:T(4,128)(2,1)} %refs_5_.1), custom_call_target="tpu_custom_call" | custom-call | tf_op jit(solution)/shard_map/pack_rows/pallas_call | solution.py:123
  3.5 30.5 %all-to-all-start = ((bf16[64,4,640]{2,1,0:T(4,128)(2,1)}), bf16[64,4,640]{2,1,0:T(4,128)(2,1)S(1)}, u32[]{:S(2)}, u32[]{:S(2)}) async-start(bf16[64,4,640]{2,1,0:T(4,128)(2,1)} %pack_rows.1), calls=%async_computation | async-start | bytes 655360 | tf_op jit(solution)/shard_map/all_to_all | solution.py:337
  34.5 1.3 reduce.3
  36.3 1.6 %copy-done = bf16[1,2,512,1024]{3,2,1,0:T(8,128)(2,1)S(1)} copy-done((bf16[1,2,512,1024]{3,2,1,0:T(8,128)(2,1)S(1)}, bf16[1,2,512,1024]{3,2,1,0:T(8,128)(2,1)}, u32[]{:S(2)}) %copy-start) | copy-done | bytes 2097176
  37.9 1.6 %copy-done.1 = bf16[1024,1024]{1,0:T(8,128)(2,1)S(1)} copy-done((bf16[1024,1024]{1,0:T(8,128)(2,1)S(1)}, bf16[1024,1024]{1,0:T(8,128)(2,1)}, u32[]{:S(2)}) %copy-start.1) | copy-done | bytes 2097176
  39.5 0.9 copy-done.2
  40.4 0.7 copy-done.5
  41.1 0.7 copy-done.8
  42.5 8.6 %encode_users.1.interest_ref = bf16[2,256,256]{2,1,0:T(8,128)(2,1)S(1)} custom-call(s32[1,2]{1,0:T(1,128)S(1)} %copy-done.9, bf16[1,2,512,1024]{3,2,1,0:T(8,128)(2,1)S(1)} %copy-done, bf16[1,2,64,1024]{3,2,1,0:T(8,128)(2,1)S(1)} %copy-done.2, bf16[1024,1024]{1,0:T(8,128)(2,1)S(1)} %copy-done.1, f32[1,1024]{1,0:T(1,128)S(1)} %bitcast.22, f32[1,256]{1,0:T(1,128)S(1)} %bitcast.23), custom_call_target="tpu_custom_call" | custom-call | tf_op jit(solution)/shard_map/encode_users/pallas_call | solution.py:67
  51.6 3.4 %collective-permute-start.2 = (bf16[24,256]{1,0:T(8,128)(2,1)S(1)}, bf16[24,256]{1,0:T(8,128)(2,1)S(1)}, u32[]{:S(2)}, u32[]{:S(2)}) collective-permute-start(bf16[24,256]{1,0:T(8,128)(2,1)S(1)} %get-tuple-element.26), channel_id=1, source_target_pairs={{0,513},{1,512},{2,515},{3,514},{4,517},{5,516},{6,519},{7,518},{8... | collective-permute-start | bytes 36872 | tf_op jit(solution)/shard_map/ppermute | solution.py:357
  55.0 2.1 %collective-permute-start.1 = (bf16[24,256]{1,0:T(8,128)(2,1)S(1)}, bf16[24,256]{1,0:T(8,128)(2,1)S(1)}, u32[]{:S(2)}, u32[]{:S(2)}) collective-permute-start(bf16[24,256]{1,0:T(8,128)(2,1)S(1)} %get-tuple-element.27), channel_id=1, source_target_pairs={{0,512},{1,513},{2,514},{3,515},{4,516},{5,517},{6,518},{7,519},{8... | collective-permute-start | bytes 36872 | tf_op jit(solution)/shard_map/ppermute | solution.py:357
  57.1 2.0 %collective-permute-start = (bf16[24,256]{1,0:T(8,128)(2,1)S(1)}, bf16[24,256]{1,0:T(8,128)(2,1)S(1)}, u32[]{:S(2)}, u32[]{:S(2)}) collective-permute-start(bf16[24,256]{1,0:T(8,128)(2,1)S(1)} %get-tuple-element.28), channel_id=1, source_target_pairs={{0,1},{1,0},{2,3},{3,2},{4,5},{5,4},{6,7},{7,6},{8,9},{9,8},{10,11... | collective-permute-start | bytes 36872 | tf_op jit(solution)/shard_map/ppermute | solution.py:357
  59.2 1.4 %collective-permute-done.2.refs_3_ = bf16[24,256]{1,0:T(8,128)(2,1)S(1)} collective-permute-done((bf16[24,256]{1,0:T(8,128)(2,1)S(1)}, bf16[24,256]{1,0:T(8,128)(2,1)S(1)}, u32[]{:S(2)}, u32[]{:S(2)}) %collective-permute-start.2) | collective-permute-done | bytes 12320 | tf_op jit(solution)/shard_map/ppermute | solution.py:357
  60.6 1.5 %collective-permute-done.refs_1_ = bf16[24,256]{1,0:T(8,128)(2,1)S(1)} collective-permute-done((bf16[24,256]{1,0:T(8,128)(2,1)S(1)}, bf16[24,256]{1,0:T(8,128)(2,1)S(1)}, u32[]{:S(2)}, u32[]{:S(2)}) %collective-permute-start) | collective-permute-done | bytes 12320 | tf_op jit(solution)/shard_map/ppermute | solution.py:357
  62.5 14.2 %all-to-all-done = bf16[64,4,640]{2,1,0:T(4,128)(2,1)S(1)} async-done(((bf16[64,4,640]{2,1,0:T(4,128)(2,1)}), bf16[64,4,640]{2,1,0:T(4,128)(2,1)S(1)}, u32[]{:S(2)}, u32[]{:S(2)}) %all-to-all-start) | async-done | bytes 327712 | tf_op jit(solution)/shard_map/all_to_all | solution.py:337
  77.3 32.5 %all_gather.3.got_ref = bf16[48,24,256]{2,1,0:T(8,128)(2,1)S(1)} all-gather(bf16[3,24,256]{2,1,0:T(8,128)(2,1)S(1)} %make_state.1), channel_id=1, replica_groups={{0,2,4,6,8,10,12,14,16,18,20,22,24,26,28,30},{1,3,5,7,9,11,13,15,17,19,..., dimensions={0}, use_global_device_ids=true | all-gather | bytes 626688 | tf_op jit(solution)/shard_map/all_gather | solution.py:362
  109.7 1.0 embed_rows.1
  110.8 14.4 %all-to-all-start.1 = ((f32[64,4,128]{2,1,0:T(4,128)}), f32[64,4,128]{2,1,0:T(4,128)S(1)}, u32[]{:S(2)}, u32[]{:S(2)}) async-start(f32[64,4,128]{2,1,0:T(4,128)} %get-tuple-element.25), calls=%async_computation.1 | async-start | bytes 262144 | tf_op jit(solution)/shard_map/all_to_all | solution.py:378
  125.2 3.4 %collective-permute-start.3 = (bf16[32,2,4,256]{3,2,1,0:T(4,128)(2,1)S(1)}, bf16[32,2,4,256]{3,2,1,0:T(4,128)(2,1)S(1)}, u32[]{:S(2)}, u32[]{:S(2)}) collective-permute-start(bf16[32,2,4,256]{3,2,1,0:T(4,128)(2,1)S(1)} %get-tuple-element.20), channel_id=1, source_target_pairs={{0,513},{1,512},{2,515},{3,514},{4,517},{5,516},{6,519},{7,518},{8... | collective-permute-start | bytes 393224 | tf_op jit(solution)/shard_map/ppermute | solution.py:390
  128.7 2.1 %collective-permute-start.4 = (bf16[32,2,4,256]{3,2,1,0:T(4,128)(2,1)S(1)}, bf16[32,2,4,256]{3,2,1,0:T(4,128)(2,1)S(1)}, u32[]{:S(2)}, u32[]{:S(2)}) collective-permute-start(bf16[32,2,4,256]{3,2,1,0:T(4,128)(2,1)S(1)} %get-tuple-element.21), channel_id=1, source_target_pairs={{0,1},{1,0},{2,3},{3,2},{4,5},{5,4},{6,7},{7,6},{8,9},{9,8},{10,11... | collective-permute-start | bytes 393224 | tf_op jit(solution)/shard_map/ppermute | solution.py:390
  130.8 2.3 %collective-permute-start.5 = (bf16[32,2,4,256]{3,2,1,0:T(4,128)(2,1)S(1)}, bf16[32,2,4,256]{3,2,1,0:T(4,128)(2,1)S(1)}, u32[]{:S(2)}, u32[]{:S(2)}) collective-permute-start(bf16[32,2,4,256]{3,2,1,0:T(4,128)(2,1)S(1)} %get-tuple-element.22), channel_id=1, source_target_pairs={{0,512},{1,513},{2,514},{3,515},{4,516},{5,517},{6,518},{7,519},{8... | collective-permute-start | bytes 393224 | tf_op jit(solution)/shard_map/ppermute | solution.py:390
  133.3 2.2 %collective-permute-done.4.refs_2_ = bf16[32,2,4,256]{3,2,1,0:T(4,128)(2,1)S(1)} collective-permute-done((bf16[32,2,4,256]{3,2,1,0:T(4,128)(2,1)S(1)}, bf16[32,2,4,256]{3,2,1,0:T(4,128)(2,1)S(1)}, u32[]{:S(2)}, u32[]{:S(2)}) %collective-permute-start.4) | collective-permute-done | bytes 131104 | tf_op jit(solution)/shard_map/ppermute | solution.py:390
  135.5 1.5 %scatter_rows.1 = (bf16[128,4,256]{2,1,0:T(4,128)(2,1)}, bf16[128,4,256]{2,1,0:T(4,128)(2,1)}) custom-call(s32[128]{0:T(128)S(1)} %reshape.17.rows_ref, bf16[32,2,4,256]{3,2,1,0:T(4,128)(2,1)S(1)} %get-tuple-element.19.refs_0_, bf16[32,2,4,256]{3,2,1,0:T(4,128)(2,1)S(1)} %collective-permute-done.3.refs_1_, ...), custom_call_target="tpu_custom_call" | custom-call | tf_op jit(solution)/shard_map/scatter_rows/pallas_call | solution.py:304
  137.0 0.7 fusion
  (38 shorter events, 3.2 us)
Async XLA Ops:
  3.5 73.2 %all-to-all-start = ((bf16[64,4,640]{2,1,0:T(4,128)(2,1)}), bf16[64,4,640]{2,1,0:T(4,128)(2,1)S(1)}, u32[]{:S(2)}, u32[]{:S(2)}) async-start(bf16[64,4,640]{2,1,0:T(4,128)(2,1)} %pack_rows.1), calls=%async_computation | async-start | bytes 655360 | tf_op jit(solution)/shard_map/all_to_all | solution.py:337
  36.3 1.6 %copy-start = (bf16[1,2,512,1024]{3,2,1,0:T(8,128)(2,1)S(1)}, bf16[1,2,512,1024]{3,2,1,0:T(8,128)(2,1)}, u32[]{:S(2)}) copy-start(bf16[1,2,512,1024]{3,2,1,0:T(8,128)(2,1)} %history_ref.1) | copy-start | bytes 6291460
  37.9 1.6 %copy-start.1 = (bf16[1024,1024]{1,0:T(8,128)(2,1)S(1)}, bf16[1024,1024]{1,0:T(8,128)(2,1)}, u32[]{:S(2)}) copy-start(bf16[1024,1024]{1,0:T(8,128)(2,1)} %weight_ref.1) | copy-start | bytes 6291460
  39.5 0.9 copy-start.2
  40.4 0.7 copy-start.5
  41.1 0.7 copy-start.8
  41.8 0.7 copy-start.9
  42.4 8.7 %copy-start.3 = (bf16[128,4,12]{0,1,2:T(4,128)(2,1)S(1)}, bf16[128,4,12]{0,1,2:T(4,128)(2,1)}, u32[]{:S(2)}) copy-start(bf16[128,4,12]{0,1,2:T(4,128)(2,1)} %param.22) | copy-start | bytes 36868
  42.4 8.7 %copy-start.4 = (bf16[128,4,12]{0,1,2:T(4,128)(2,1)S(1)}, bf16[128,4,12]{0,1,2:T(4,128)(2,1)}, u32[]{:S(2)}) copy-start(bf16[128,4,12]{0,1,2:T(4,128)(2,1)} %param.23) | copy-start | bytes 36868
  42.5 8.7 %copy-start.6 = (bf16[4,12]{1,0:T(4,128)(2,1)S(1)}, bf16[4,12]{1,0:T(4,128)(2,1)}, u32[]{:S(2)}) copy-start(bf16[4,12]{1,0:T(4,128)(2,1)} %refs_4_.1) | copy-start | bytes 292
  42.5 8.7 %copy-start.7 = (bf16[4,12]{1,0:T(4,128)(2,1)S(1)}, bf16[4,12]{1,0:T(4,128)(2,1)}, u32[]{:S(2)}) copy-start(bf16[4,12]{1,0:T(4,128)(2,1)} %refs_5_.1) | copy-start | bytes 292
  51.6 9.0 %collective-permute-start.2 = (bf16[24,256]{1,0:T(8,128)(2,1)S(1)}, bf16[24,256]{1,0:T(8,128)(2,1)S(1)}, u32[]{:S(2)}, u32[]{:S(2)}) collective-permute-start(bf16[24,256]{1,0:T(8,128)(2,1)S(1)} %get-tuple-element.26), channel_id=1, source_target_pairs={{0,513},{1,512},{2,515},{3,514},{4,517},{5,516},{6,519},{7,518},{8... | collective-permute-start | bytes 36872 | tf_op jit(solution)/shard_map/ppermute | solution.py:357
  55.0 5.6 %collective-permute-start.1 = (bf16[24,256]{1,0:T(8,128)(2,1)S(1)}, bf16[24,256]{1,0:T(8,128)(2,1)S(1)}, u32[]{:S(2)}, u32[]{:S(2)}) collective-permute-start(bf16[24,256]{1,0:T(8,128)(2,1)S(1)} %get-tuple-element.27), channel_id=1, source_target_pairs={{0,512},{1,513},{2,514},{3,515},{4,516},{5,517},{6,518},{7,519},{8... | collective-permute-start | bytes 36872 | tf_op jit(solution)/shard_map/ppermute | solution.py:357
  57.1 5.0 %collective-permute-start = (bf16[24,256]{1,0:T(8,128)(2,1)S(1)}, bf16[24,256]{1,0:T(8,128)(2,1)S(1)}, u32[]{:S(2)}, u32[]{:S(2)}) collective-permute-start(bf16[24,256]{1,0:T(8,128)(2,1)S(1)} %get-tuple-element.28), channel_id=1, source_target_pairs={{0,1},{1,0},{2,3},{3,2},{4,5},{5,4},{6,7},{7,6},{8,9},{9,8},{10,11... | collective-permute-start | bytes 36872 | tf_op jit(solution)/shard_map/ppermute | solution.py:357
  110.8 26.2 %all-to-all-start.1 = ((f32[64,4,128]{2,1,0:T(4,128)}), f32[64,4,128]{2,1,0:T(4,128)S(1)}, u32[]{:S(2)}, u32[]{:S(2)}) async-start(f32[64,4,128]{2,1,0:T(4,128)} %get-tuple-element.25), calls=%async_computation.1 | async-start | bytes 262144 | tf_op jit(solution)/shard_map/all_to_all | solution.py:378
  125.2 8.0 %collective-permute-start.3 = (bf16[32,2,4,256]{3,2,1,0:T(4,128)(2,1)S(1)}, bf16[32,2,4,256]{3,2,1,0:T(4,128)(2,1)S(1)}, u32[]{:S(2)}, u32[]{:S(2)}) collective-permute-start(bf16[32,2,4,256]{3,2,1,0:T(4,128)(2,1)S(1)} %get-tuple-element.20), channel_id=1, source_target_pairs={{0,513},{1,512},{2,515},{3,514},{4,517},{5,516},{6,519},{7,518},{8... | collective-permute-start | bytes 393224 | tf_op jit(solution)/shard_map/ppermute | solution.py:390
  128.7 6.8 %collective-permute-start.4 = (bf16[32,2,4,256]{3,2,1,0:T(4,128)(2,1)S(1)}, bf16[32,2,4,256]{3,2,1,0:T(4,128)(2,1)S(1)}, u32[]{:S(2)}, u32[]{:S(2)}) collective-permute-start(bf16[32,2,4,256]{3,2,1,0:T(4,128)(2,1)S(1)} %get-tuple-element.21), channel_id=1, source_target_pairs={{0,1},{1,0},{2,3},{3,2},{4,5},{5,4},{6,7},{7,6},{8,9},{9,8},{10,11... | collective-permute-start | bytes 393224 | tf_op jit(solution)/shard_map/ppermute | solution.py:390
  130.8 4.7 %collective-permute-start.5 = (bf16[32,2,4,256]{3,2,1,0:T(4,128)(2,1)S(1)}, bf16[32,2,4,256]{3,2,1,0:T(4,128)(2,1)S(1)}, u32[]{:S(2)}, u32[]{:S(2)}) collective-permute-start(bf16[32,2,4,256]{3,2,1,0:T(4,128)(2,1)S(1)} %get-tuple-element.22), channel_id=1, source_target_pairs={{0,512},{1,513},{2,514},{3,515},{4,516},{5,517},{6,518},{7,519},{8... | collective-permute-start | bytes 393224 | tf_op jit(solution)/shard_map/ppermute | solution.py:390
